TPU v7x, 512 devices: a whole 4x4x16 slice. The times are simulated.
512 devices in a mesh: expert: 8 (over y, core), etensor: 16 (over z), dp: 4 (over x).
Axes of the slice: x: 4, y: 4, z: 16, core: 2. Of those that a mesh axis runs over, the one named last changes fastest.
Arguments:
- tokens: bfloat16 [4096, 4096], P(('expert', 'dp'), 'etensor'), may hold values from -6 to 6
- out_grad: bfloat16 [4096, 4096], P(('expert', 'dp'), 'etensor'), may hold values from -6 to 6
- routes: int32 [4096, 2], P(('expert', 'dp')), may hold values from 0 to 7, all different within a row; in each aligned block of 128 rows (0 to 127, 128 to 255, ...) at most 36 rows name the same one
- gate_probs: float32 [4096, 2], P(('expert', 'dp')), may hold values from 0.1 to 1
- gate_weight: bfloat16 [8, 4096, 8192], P('expert', 'dp', 'etensor'), may hold values from -0.09375 to 0.09375
- up_weight: bfloat16 [8, 4096, 8192], P('expert', 'dp', 'etensor'), may hold values from -0.09375 to 0.09375
- down_weight: bfloat16 [8, 8192, 4096], P('expert', 'etensor', 'dp'), may hold values from -0.0625 to 0.0625
Outputs:
- input_grad: bfloat16 [4096, 4096], P(('expert', 'dp'), 'etensor')
- gate_grad: float32 [4096, 2], P(('expert', 'dp'))
Inputs may be any that keep to these rules, and one draw needn't show every extreme that they name: `routes`: the two experts of a token differ. Within the 128 rows of one token group no expert is named by more than 36 rows, and in some group some expert is named by exactly 36 rows.
All inputs are finite; a program needn't handle non-finite values.
Results may differ from a plain program's by a relative error of at most 0.024.
Values may be sent and summed in bfloat16 or wider, within the bound.
No kernel may reach another device: no remote copies, remote signals or barrier semaphores. Data moves between devices by JAX's collectives and lax.ppermute only.
A program may use at most 64 MiB of HBM per device.

v0:
```python
import jax
import jax.numpy as jnp
from jax import lax
from jax.sharding import PartitionSpec as P


def shards(tokens, out_grad, routes, gate_probs, gate_weight, up_weight, down_weight):
    tok_rows = tokens.shape[0]
    owners = lax.axis_size("expert")
    experts = owners * gate_weight.shape[0]
    capacity = min(tok_rows, 9 * tok_rows // (4 * experts))
    flat_routes = routes.reshape(-1)
    onehot = (flat_routes[:, None] == jnp.arange(experts, dtype=jnp.int32)[None, :]).astype(
        jnp.int32
    )
    ranks = jnp.cumsum(onehot, axis=0) - onehot
    slot = jnp.sum(ranks * onehot, axis=1)
    position = flat_routes * capacity + slot
    dispatch = (
        jnp.arange(experts * capacity, dtype=jnp.int32)[:, None] == position[None, :]
    ).astype(jnp.bfloat16)

    def place(rows):
        doubled = jnp.repeat(rows, 2, axis=0)
        placed = jnp.dot(dispatch, doubled, preferred_element_type=jnp.float32).astype(jnp.bfloat16)
        return placed.reshape(experts, capacity, rows.shape[1])

    part_x, part_dy = (
        lax.all_to_all(place(tokens), "expert", split_axis=0, concat_axis=0, tiled=True),
        lax.all_to_all(place(out_grad), "expert", split_axis=0, concat_axis=0, tiled=True),
    )
    recv_x, recv_dy = (
        lax.all_gather(part_x, "etensor", axis=2, tiled=True),
        lax.all_gather(part_dy, "etensor", axis=2, tiled=True),
    )
    width = recv_x.shape[2]
    rows = recv_x.reshape(-1, width)
    grads = recv_dy.reshape(-1, width)
    contract = (((1,), (1,)), ((), ()))
    w_gate, w_up, w_down = (
        lax.all_gather(gate_weight, "dp", axis=1, tiled=True),
        lax.all_gather(up_weight, "dp", axis=1, tiled=True),
        lax.all_gather(down_weight, "dp", axis=2, tiled=True),
    )
    w_gate = w_gate[0]
    w_up = w_up[0]
    w_down = w_down[0]
    gate_pre = jnp.dot(rows, w_gate, preferred_element_type=jnp.float32)
    up_pre = jnp.dot(rows, w_up, preferred_element_type=jnp.float32)
    back = lax.dot_general(grads, w_down, contract, preferred_element_type=jnp.float32)
    sig = jax.nn.sigmoid(gate_pre)
    act = gate_pre * sig
    hidden = act * up_pre
    gate_part = jnp.sum(hidden * back, axis=1)
    d_gate = (back * up_pre * sig * (1.0 + gate_pre * (1.0 - sig))).astype(jnp.bfloat16)
    d_up = (back * act).astype(jnp.bfloat16)
    term = lax.dot_general(d_gate, w_gate, contract, preferred_element_type=jnp.float32)
    term = term + lax.dot_general(d_up, w_up, contract, preferred_element_type=jnp.float32)
    input_rows = lax.psum_scatter(
        term.astype(jnp.bfloat16), "etensor", scatter_dimension=1, tiled=True
    )
    gate_rows = lax.psum(gate_part, "etensor")
    slice_width = input_rows.shape[1]
    back_rows = lax.all_to_all(
        input_rows.reshape(owners, capacity, slice_width),
        "expert",
        split_axis=0,
        concat_axis=0,
        tiled=True,
    )
    back_gate = lax.all_to_all(
        gate_rows.reshape(owners, capacity), "expert", split_axis=0, concat_axis=0, tiled=True
    )
    picked = jnp.take(back_rows.reshape(experts * capacity, slice_width), position, axis=0)
    picked_gate = jnp.take(back_gate.reshape(experts * capacity), position, axis=0)
    probs = gate_probs.reshape(-1)
    weighted = picked.astype(jnp.float32) * probs[:, None]
    input_grad = jnp.sum(weighted.reshape(tok_rows, 2, slice_width), axis=1).astype(jnp.bfloat16)
    return (input_grad, picked_gate.reshape(tok_rows, 2))


def solution(mesh):
    return jax.shard_map(
        shards,
        mesh=mesh,
        in_specs=(
            P(("expert", "dp"), "etensor"),
            P(("expert", "dp"), "etensor"),
            P(("expert", "dp"), None),
            P(("expert", "dp"), None),
            P("expert", "dp", "etensor"),
            P("expert", "dp", "etensor"),
            P("expert", "etensor", "dp"),
        ),
        out_specs=(P(("expert", "dp"), "etensor"), P(("expert", "dp"), None)),
        check_vma=False,
    )
```

profile of v0, /device:TPU:1, one launch (start us, length us, event | category | flops | bytes accessed | tf_op | source)
XLA Modules:
  0.0 464.1 jit_solution(105573610856387060)
XLA Ops:
  7.2 0.8 copy.11
  8.0 0.1 eq.39
  8.1 0.1 reshape.115
  8.3 0.6 reduce-window.6
  8.9 0.2 slice_reduce_fusion
  9.1 0.1 fusion.16
  9.2 0.9 broadcast_in_dim.27
  10.2 0.2 convolution_convert_fusion
  10.5 15.5 %all_to_all.24 = bf16[8,36,256]{2,1,0:T(8,128)(2,1)} all-to-all(bf16[8,36,256]{2,1,0:T(8,128)(2,1)S(1)} %reshape.121), channel_id=1, replica_groups=mesh['expert'=8,'etensor'=16,'dp'=4] {'expert'}, dimensions={0} | all-to-all | bytes 294912 | tf_op jit(solution)/shard_map/all_to_all | solution.py:29
  26.0 0.9 broadcast_in_dim.26
  27.0 0.2 convolution_convert_fusion.1
  27.3 9.5 %all_to_all.25 = bf16[8,36,256]{2,1,0:T(8,128)(2,1)} all-to-all(bf16[8,36,256]{2,1,0:T(8,128)(2,1)S(1)} %reshape.118), channel_id=1, replica_groups=mesh['expert'=8,'etensor'=16,'dp'=4] {'expert'}, dimensions={0} | all-to-all | bytes 294912 | tf_op jit(solution)/shard_map/all_to_all | solution.py:30
  36.9 0.7 all-gather.14.cloned.1.call-update
  37.6 0.5 all-gather.12.cloned.1.call-update
  38.2 0.5 all-gather.8.cloned.1.call-update
  38.8 59.3 %all-gather.10.cloned.1.call-done = bf16[8,36,4096]{2,1,0:T(8,128)(2,1)} async-done(((bf16[8,36,256]{2,1,0:T(8,128)(2,1)}), bf16[8,36,4096]{2,1,0:T(8,128)(2,1)}) %all-gather.10.cloned.1.call-update) | async-done | bytes 2359312 | tf_op jit(solution)/shard_map/all_gather | solution.py:33
  98.1 4.1 reshape.122
  102.2 76.2 %all-gather.6.cloned.1.call-done = bf16[8,36,4096]{2,1,0:T(8,128)(2,1)} async-done(((bf16[8,36,256]{2,1,0:T(8,128)(2,1)}), bf16[8,36,4096]{2,1,0:T(8,128)(2,1)}) %all-gather.6.cloned.1.call-update) | async-done | bytes 2359312 | tf_op jit(solution)/shard_map/all_gather | solution.py:34
  178.4 2.7 reshape.119
  181.1 60.3 %all-gather.14.cloned.1.call-done = bf16[1,4096,512]{2,1,0:T(8,128)(2,1)} async-done(((bf16[1,1024,512]{2,1,0:T(8,128)(2,1)}), bf16[1,4096,512]{2,1,0:T(8,128)(2,1)}) %all-gather.14.cloned.1.call-update) | async-done | bytes 4194320 | tf_op jit(solution)/shard_map/all_gather | solution.py:41
  241.4 4.3 fusion.3
  245.7 54.0 %all-gather.12.cloned.1.call-done = bf16[1,4096,512]{2,1,0:T(8,128)(2,1)} async-done(((bf16[1,1024,512]{2,1,0:T(8,128)(2,1)}), bf16[1,4096,512]{2,1,0:T(8,128)(2,1)}) %all-gather.12.cloned.1.call-update) | async-done | bytes 4194320 | tf_op jit(solution)/shard_map/all_gather | solution.py:42
  299.7 5.1 %fusion.6 = f32[288,512]{1,0:T(8,128)} fusion(bf16[288,4096]{1,0:T(8,128)(2,1)} %reshape.122, bf16[1,4096,512]{2,1,0:T(8,128)(2,1)} %all-gather.12.cloned.1.call-done), kind=kOutput, calls=%fused_computation.9 | convolution fusion | flops 1207959552 | bytes 7143424 | tf_op jit(solution)/shard_map/dot_general | solution.py:49
  304.9 53.2 %all-gather.8.cloned.1.call-done = bf16[1,512,4096]{2,1,0:T(8,128)(2,1)} async-done(((bf16[1,512,1024]{2,1,0:T(8,128)(2,1)}), bf16[1,512,4096]{2,1,0:T(8,128)(2,1)}) %all-gather.8.cloned.1.call-update) | async-done | bytes 4194320 | tf_op jit(solution)/shard_map/all_gather | solution.py:43
  358.0 4.0 multiply_reduce_fusion
  362.1 1.5 fusion.1
  363.6 0.6 copy-done.1
  364.3 2.9 fusion
  367.2 0.1 mul.75
  367.4 0.1 all_to_all.18
  367.5 25.3 %psum.7 = f32[8,1,36]{2,1,0:T(1,128)} all-reduce(f32[8,1,36]{2,1,0:T(1,128)S(1)} %all_to_all.18), channel_id=1, replica_groups=mesh['expert'=8,'etensor'=16,'dp'=4] {'etensor'}, use_global_device_ids=true, to_apply=%region_6.7 | all-reduce | flops 288 | bytes 2304 | tf_op jit(solution)/shard_map/psum | solution.py:62
  392.8 11.7 %all-to-all-start.3 = ((f32[8,1,36]{2,1,0:T(1,128)}), f32[8,1,36]{2,1,0:T(1,128)S(1)}, u32[]{:S(2)}, u32[]{:S(2)}) async-start(f32[8,1,36]{2,1,0:T(1,128)} %psum.7), calls=%async_computation.4 | async-start | bytes 8192 | tf_op jit(solution)/shard_map/all_to_all | solution.py:71
  404.5 0.1 reduce_sum.32
  404.6 0.1 copy.14
  404.7 4.2 all-to-all-done.3
  409.0 0.5 broadcast.98
  409.5 0.7 reduce.5
  410.1 0.1 reshape.125
  410.2 1.9 gather_fusion.1
  412.2 0.1 gather.15
  412.3 19.7 %reduce-scatter.2.cloned.1.call-done = bf16[288,256]{1,0:T(8,128)(2,1)} async-done(((bf16[288,4096]{1,0:T(8,128)(2,1)}), bf16[288,256]{1,0:T(8,128)(2,1)}) %reduce-scatter.2.cloned.1.call-update) | async-done | bytes 147472 | tf_op jit(solution)/shard_map/reduce_scatter | solution.py:59
  432.0 1.6 reshape.123
  433.6 15.0 %all-to-all-start.2 = ((bf16[8,36,256]{2,1,0:T(8,128)(2,1)}), bf16[8,36,256]{2,1,0:T(8,128)(2,1)S(1)}, u32[]{:S(2)}, u32[]{:S(2)}) async-start(bf16[8,36,256]{2,1,0:T(8,128)(2,1)} %reshape.123), calls=%async_computation.3 | async-start | bytes 327680 | tf_op jit(solution)/shard_map/all_to_all | solution.py:64
  448.7 0.6 copy.15
  449.3 4.9 %all-to-all-done.2 = bf16[8,36,256]{2,1,0:T(8,128)(2,1)S(1)} async-done(((bf16[8,36,256]{2,1,0:T(8,128)(2,1)}), bf16[8,36,256]{2,1,0:T(8,128)(2,1)S(1)}, u32[]{:S(2)}, u32[]{:S(2)}) %all-to-all-start.2) | async-done | bytes 147488 | tf_op jit(solution)/shard_map/all_to_all | solution.py:64
  454.2 1.2 gather_fusion
  455.4 0.1 gather.13
  455.5 1.8 multiply_reduce_fusion.1
  (29 shorter events, 0.6 us)
Async XLA Ops:
  7.2 91.0 %all-gather.10.cloned.1.call-start = ((), (), s32[]{:S(2)}) async-start(), calls=%async_computation.7 | async-start | bytes 2785280 | tf_op jit(solution)/shard_map/all_gather | solution.py:33
  26.0 152.4 %all-gather.6.cloned.1.call-start = ((), (), s32[]{:S(2)}) async-start(), calls=%async_computation.5 | async-start | bytes 2785280 | tf_op jit(solution)/shard_map/all_gather | solution.py:34
  36.8 204.6 %all-gather.14.cloned.1.call-start = ((), (), s32[]{:S(2)}) async-start(), calls=%async_computation.9 | async-start | bytes 5242880 | tf_op jit(solution)/shard_map/all_gather | solution.py:41
  37.6 262.2 %all-gather.12.cloned.1.call-start = ((), (), s32[]{:S(2)}) async-start(), calls=%async_computation.8 | async-start | bytes 5242880 | tf_op jit(solution)/shard_map/all_gather | solution.py:42
  38.1 319.9 %all-gather.8.cloned.1.call-start = ((), (), s32[]{:S(2)}) async-start(), calls=%async_computation.6 | async-start | bytes 5242880 | tf_op jit(solution)/shard_map/all_gather | solution.py:43
  38.7 393.3 %reduce-scatter.2.cloned.1.call-start = ((), (), s32[]{:S(2)}) async-start(), calls=%async_computation.10 | async-start | bytes 2506752 | tf_op jit(solution)/shard_map/reduce_scatter | solution.py:59
  358.0 4.0 copy-start
  358.0 4.0 copy-start.2
  362.1 2.2 copy-start.1
  364.3 40.3 %copy-start.3 = (f32[128,2]{0,1:T(2,128)S(1)}, f32[128,2]{0,1:T(2,128)}, u32[]{:S(2)}) copy-start(f32[128,2]{0,1:T(2,128)} %param.10) | copy-start | bytes 3076
  392.8 16.2 %all-to-all-start.3 = ((f32[8,1,36]{2,1,0:T(1,128)}), f32[8,1,36]{2,1,0:T(1,128)S(1)}, u32[]{:S(2)}, u32[]{:S(2)}) async-start(f32[8,1,36]{2,1,0:T(1,128)} %psum.7), calls=%async_computation.4 | async-start | bytes 8192 | tf_op jit(solution)/shard_map/all_to_all | solution.py:71
  433.6 20.6 %all-to-all-start.2 = ((bf16[8,36,256]{2,1,0:T(8,128)(2,1)}), bf16[8,36,256]{2,1,0:T(8,128)(2,1)S(1)}, u32[]{:S(2)}, u32[]{:S(2)}) async-start(bf16[8,36,256]{2,1,0:T(8,128)(2,1)} %reshape.123), calls=%async_computation.3 | async-start | bytes 327680 | tf_op jit(solution)/shard_map/all_to_all | solution.py:64
Sparse Core Ops, SparseCore 0:
  26.1 71.9 all-gather.9
  100.1 78.2 all-gather.5
  180.5 60.8 all-gather.13
  243.4 56.3 all-gather.11
  301.7 56.2 all-gather.7
  367.3 64.6 reduce-scatter.1
where the time goes:
time: 465 us; the launch traced here: 464 us
  waiting for transfers between devices  334 us (72%)
  blocking collectives  50.4 us (11%)
  starting transfers between devices  26.9 us (6%)
  matrix products  18.3 us (4%)
  local copies, waits for them, and re-layouts  17.4 us (4%)
  between operations  14.3 us (3%)
    all_gather x1, waiting for transfers between devices, shards(): lax.all_gather(part_dy, 'etensor', axis=2, tiled=True)  76.2 us
    all_gather x1, waiting for transfers between devices, shards(): lax.all_gather(gate_weight, 'dp', axis=1, tiled=True)  60.3 us
    all_gather x1, waiting for transfers between devices, shards(): lax.all_gather(part_x, 'etensor', axis=2, tiled=True)  59.3 us
    all_gather x1, waiting for transfers between devices, shards(): lax.all_gather(up_weight, 'dp', axis=1, tiled=True)  54 us
    all_gather x1, waiting for transfers between devices, shards(): lax.all_gather(down_weight, 'dp', axis=2, tiled=True)  53.2 us
    psum x1, blocking collectives, shards(): gate_rows = lax.psum(gate_part, 'etensor')  25.3 us
    reduce_scatter x1, waiting for transfers between devices, shards(): lax.psum_scatter(term.astype(jnp.bfloat16), 'etensor', scatter_dimension=...  19.7 us
    all_to_all x1, blocking collectives, shards(): lax.all_to_all(place(tokens), 'expert', split_axis=0, concat_axis=0, tile...  15.5 us
  transfers between devices with their start and end apart: 8, of which 8 were waited for; matrix products, arithmetic and copies ran while one was open for 5% of the time, Pallas kernels for 0%

commit v1 on v0

v1 whole, which is shorter than its diff:
```python
import functools

import jax
import jax.numpy as jnp
from jax import lax
from jax.experimental import pallas as pl
from jax.experimental.pallas import tpu as pltpu
from jax.sharding import PartitionSpec as P

NT = (((1,), (1,)), ((), ()))


def expert_kernel(feat, ff, cap_rows, blocks, pitch, slots, slot_of, order, z_of, recv, *refs):
    weights, (out, rows_v, wg, wu, wd, sems) = refs[:15], refs[15:]
    per = blocks // 4
    half = wg.shape[1] // 2
    half_ff = wd.shape[1] // 2
    copies = []

    def start(src, dst):
        copy = pltpu.make_async_copy(src, dst, sems.at[len(copies)])
        copy.start()
        copies.append(copy)
        return copy

    waits = []
    for s in range(4):
        group = [start(recv.at[pl.ds(slot_of[s] * per, per)], rows_v.at[s])]
        if s < 3:
            g, u, d = weights[3 * s : 3 * s + 3]
            group += [start(g.at[0], wg.at[s]), start(u.at[0], wu.at[s]), start(d.at[0], wd.at[s])]
        else:
            g1, u1, d1, g2, u2, d2 = weights[9:]
            group += [
                start(g1, wg.at[s, pl.ds(0, half)]),
                start(u1, wu.at[s, pl.ds(0, half)]),
                start(d1, wd.at[s, pl.ds(0, half_ff)]),
                start(g2, wg.at[s, pl.ds(half, half)]),
                start(u2, wu.at[s, pl.ds(half, half)]),
                start(d2, wd.at[s, pl.ds(half_ff, half_ff)]),
            ]
        waits.append(group)

    gate_pre = up_pre = back = None
    for s in range(4):
        for copy in waits[s]:
            copy.wait()
        x = jnp.concatenate([rows_v[s, k, :, :feat] for k in range(per)], axis=1)
        y = jnp.concatenate([rows_v[s, k, :, feat:] for k in range(per)], axis=1)
        g = jnp.dot(x, wg[s], preferred_element_type=jnp.float32)
        u = jnp.dot(x, wu[s], preferred_element_type=jnp.float32)
        b = lax.dot_general(y, wd[s], NT, preferred_element_type=jnp.float32)
        gate_pre = g if s == 0 else gate_pre + g
        up_pre = u if s == 0 else up_pre + u
        back = b if s == 0 else back + b

    sig = 1.0 / (1.0 + jnp.exp(-gate_pre))
    act = gate_pre * sig
    prod = act * up_pre * back
    d_gate = (back * up_pre * sig * (1.0 + gate_pre * (1.0 - sig))).astype(jnp.bfloat16)
    d_up = (back * act).astype(jnp.bfloat16)

    ones = jnp.ones((16, prod.shape[1]), jnp.bfloat16)
    total = None
    rest = prod
    for _ in range(3):
        limb = rest.astype(jnp.bfloat16)
        rest = rest - limb.astype(jnp.float32)
        part = lax.dot_general(ones, limb, NT, preferred_element_type=jnp.float32)
        total = part if total is None else total + part
    top = total.astype(jnp.bfloat16).astype(jnp.float32)
    low = total - top
    over = cap_rows - feat
    row = lax.broadcasted_iota(jnp.int32, (16, feat), 0)
    lane = lax.broadcasted_iota(jnp.int32, (16, feat), 1)
    q = z_of[0]
    mine = (lane >= q * over) & (lane < (q + 1) * over)
    wide = lambda v: jnp.concatenate([v[:, feat:]] * (feat // over), axis=1)
    extra = jnp.where(row == q, top[:, :feat], 0.0)
    extra = jnp.where(row == q + slots, low[:, :feat], extra)
    extra = jnp.where((row == 2 * slots) & mine, wide(top), extra)
    extra = jnp.where((row == 2 * slots + 1) & mine, wide(low), extra)
    extra = extra.astype(jnp.bfloat16)
    for z in range(blocks):
        out[pl.ds(pitch * z + cap_rows, 16), :] = extra
        if pitch > cap_rows + 16 and pitch * (z + 1) <= out.shape[0]:
            out[pl.ds(pitch * z + cap_rows + 16, pitch - cap_rows - 16), :] = jnp.zeros(
                (pitch - cap_rows - 16, feat), jnp.bfloat16
            )
    for s in range(4):
        term = lax.dot_general(d_gate, wg[s], NT, preferred_element_type=jnp.float32)
        term = term + lax.dot_general(d_up, wu[s], NT, preferred_element_type=jnp.float32)
        for k in range(per):
            at = pl.multiple_of((slot_of[s] * per + k) * pitch, 16)
            out[pl.ds(at, cap_rows), :] = term[:, k * feat : (k + 1) * feat].astype(jnp.bfloat16)


def expert_part(recv, weights, x_index, z_index, pitch, out_rows, slots):
    blocks, cap_rows, both = recv.shape
    feat = both // 2
    ff = weights[0].shape[2]
    depth = weights[0].shape[1]
    slot_of = jnp.stack([x_index, (x_index + 3) % 4, (x_index + 1) % 4, (x_index + 2) % 4])
    order = slot_of
    z_of = jnp.reshape(z_index % slots, (1,)).astype(jnp.int32)
    smem = pl.BlockSpec(memory_space=pltpu.SMEM)
    return pl.pallas_call(
        functools.partial(expert_kernel, feat, ff, cap_rows, blocks, pitch, slots),
        out_shape=jax.ShapeDtypeStruct((out_rows, feat), jnp.bfloat16),
        in_specs=[smem, smem, smem] + [pl.BlockSpec(memory_space=pl.ANY)] * 16,
        out_specs=pl.BlockSpec(memory_space=pltpu.VMEM),
        scratch_shapes=[
            pltpu.VMEM((4, blocks // 4, cap_rows, both), jnp.bfloat16),
            pltpu.VMEM((4, depth, ff), jnp.bfloat16),
            pltpu.VMEM((4, depth, ff), jnp.bfloat16),
            pltpu.VMEM((4, ff, depth), jnp.bfloat16),
            pltpu.SemaphoreType.DMA((19,)),
        ],
        compiler_params=pltpu.CompilerParams(vmem_limit_bytes=48 * 1024 * 1024),
        cost_estimate=pl.CostEstimate(
            flops=10 * cap_rows * 4 * depth * ff, bytes_accessed=24 << 20, transcendentals=cap_rows * ff
        ),
    )(slot_of.astype(jnp.int32), order.astype(jnp.int32), z_of, recv, *weights)


def shift(value, axis, step):
    size = lax.axis_size(axis)
    return lax.ppermute(value, axis, [(i, (i + step) % size) for i in range(size)])


def shards(tokens, out_grad, routes, gate_probs, gate_weight, up_weight, down_weight):
    tok_rows, feat = tokens.shape
    owners = lax.axis_size("expert")
    blocks = lax.axis_size("etensor")
    experts = owners * gate_weight.shape[0]
    capacity = min(tok_rows, 9 * tok_rows // (4 * experts))
    x_index = lax.axis_index("dp")
    z_index = lax.axis_index("etensor")
    cap_rows = owners * capacity
    slots = 7

    own = (gate_weight, up_weight, down_weight)
    left = tuple(shift(w, "dp", 1) for w in own)
    right = tuple(shift(w, "dp", -1) for w in own)
    far_left = tuple(shift(w[0, : w.shape[1] // 2], "dp", 1) for w in left)
    far_right = tuple(shift(w[0, w.shape[1] // 2 :], "dp", -1) for w in right)

    expert_ids = jnp.arange(experts, dtype=jnp.int32)
    hot = ((routes[:, :1] == expert_ids) | (routes[:, 1:] == expert_ids)).astype(jnp.bfloat16)
    earlier = jnp.tril(jnp.ones((tok_rows, tok_rows), jnp.bfloat16), -1)
    ranks = jnp.dot(earlier, hot, preferred_element_type=jnp.float32).astype(jnp.int32)
    slot = jnp.stack(
        [jnp.sum(jnp.where(routes[:, k : k + 1] == expert_ids, ranks, 0), axis=1) for k in range(2)],
        axis=1,
    )
    position = routes * capacity + slot
    places = jnp.arange(cap_rows, dtype=jnp.int32)[:, None]
    dispatch = ((places == position[None, :, 0]) | (places == position[None, :, 1])).astype(
        jnp.bfloat16
    )
    both = jnp.concatenate([tokens, out_grad], axis=1)
    placed = jnp.dot(dispatch, both, preferred_element_type=jnp.float32).astype(jnp.bfloat16)
    part = lax.all_to_all(
        placed.reshape(experts, capacity, 2 * feat), "expert", split_axis=0, concat_axis=0, tiled=True
    )
    recv = lax.all_gather(part.reshape(cap_rows, 2 * feat), "etensor", axis=0, tiled=False)

    pitch = PITCH
    out_rows = blocks * pitch if ALIGNED else blocks * (pitch - 1)
    terms = expert_part(
        recv, own + left + right + far_left + far_right, x_index, z_index, pitch, out_rows, slots
    )
    summed = lax.psum_scatter(terms, "etensor", scatter_dimension=0, tiled=True)
    if not ALIGNED:
        summed = lax.dynamic_slice_in_dim(summed, z_index, cap_rows + 16, 0)
    extra = summed[cap_rows:].astype(jnp.float32)
    over = cap_rows - feat
    head = jnp.sum(extra[: 2 * slots], axis=0)
    tail = jnp.sum(extra[2 * slots :].reshape(2, feat // over, over)[:, :slots], axis=(0, 1))
    gate_rows = jnp.concatenate([head, tail])
    gate_top = gate_rows.astype(jnp.bfloat16)
    gate_low = (gate_rows - gate_top.astype(jnp.float32)).astype(jnp.bfloat16)
    gates = jnp.concatenate(
        [
            gate_top.reshape(owners, 1, capacity),
            gate_low.reshape(owners, 1, capacity),
            jnp.zeros((owners, 1, feat - 2 * capacity), jnp.bfloat16),
        ],
        axis=2,
    )
    payload = jnp.concatenate([summed[:cap_rows].reshape(owners, capacity, feat), gates], axis=1)
    came = lax.all_to_all(payload, "expert", split_axis=0, concat_axis=0, tiled=True)
    came_rows = came[:, :capacity].reshape(cap_rows, feat)
    came_gate = (
        came[:, capacity, :capacity].astype(jnp.float32)
        + came[:, capacity, capacity : 2 * capacity].astype(jnp.float32)
    ).reshape(cap_rows)
    flat = position.reshape(-1)
    picked = jnp.take(came_rows, flat, axis=0, mode="clip")
    picked_gate = jnp.take(came_gate, flat, axis=0, mode="clip")
    weighted = picked.astype(jnp.float32) * gate_probs.reshape(-1)[:, None]
    input_grad = jnp.sum(weighted.reshape(tok_rows, 2, feat), axis=1).astype(jnp.bfloat16)
    return (input_grad, picked_gate.reshape(tok_rows, 2))


PITCH = 320
ALIGNED = False


def solution(mesh):
    return jax.shard_map(
        shards,
        mesh=mesh,
        in_specs=(
            P(("expert", "dp"), "etensor"),
            P(("expert", "dp"), "etensor"),
            P(("expert", "dp"), None),
            P(("expert", "dp"), None),
            P("expert", "dp", "etensor"),
            P("expert", "dp", "etensor"),
            P("expert", "etensor", "dp"),
        ),
        out_specs=(P(("expert", "dp"), "etensor"), P(("expert", "dp"), None)),
        check_vma=False,
    )
```

time: 465 us -> 324 us (0.70)
  waiting for transfers between devices: 334 us -> 214 us
  blocking collectives: 50.4 us -> 16.8 us
  starting transfers between devices: 26.9 us -> 46.7 us
  matrix products: 18.3 us -> 1.3 us
  Pallas kernels: 0 us -> 12.3 us
    all_gather x5 -> x1, waiting for transfers between devices: 303 us -> 0.01 us  [shards(): lax.all_gather(part.reshape(cap_rows, 2 * feat), 'etensor', axis=0, tiled...]
    unnamed x6 -> x3, waiting for transfers between devices: 1.79 us -> 137 us
    ppermute x0 -> x12, waiting for transfers between devices: none -> 71.9 us  [shift(): lax.ppermute(value, axis, [(i, (i + step) % size) for i in range(size)])]
    ppermute x0 -> x12, starting transfers between devices: none -> 33.2 us  [shift(): lax.ppermute(value, axis, [(i, (i + step) % size) for i in range(size)])]
    psum x1 -> x0, blocking collectives: 25.3 us -> none  [shards(): gate_rows = lax.psum(gate_part, 'etensor')]
    reduce_scatter x1 -> x0, waiting for transfers between devices: 19.7 us -> none  [shards(): lax.psum_scatter(term.astype(jnp.bfloat16), 'etensor', scatter_dimension=...]
    dot_general x7 -> x2, matrix products: 18.3 us -> 1.3 us  [the longest x1 1.09 us: shards(): jnp.dot(dispatch, both, preferred_element_type=jnp.float32)]
    all_to_all x2 -> x1, starting transfers between devices: 26.7 us -> 13.4 us  [shards(): lax.all_to_all(payload, 'expert', split_axis=0, concat_axis=0, tiled=True)]
  transfers between devices with their start and end apart: 8 -> 15, of which waited for: 8 -> 8; matrix products, arithmetic and copies ran while one was open for 5% -> 2% of each run, Pallas kernels for 0% -> 0%
where the time goes in v1:
time: 324 us; the launch traced here: 323 us
  waiting for transfers between devices  214 us (66%)
  starting transfers between devices  46.7 us (14%)
  blocking collectives  16.8 us (5%)
  between operations  15 us (5%)
  local copies, waits for them, and re-layouts  12.9 us (4%)
  Pallas kernels  12.3 us (4%)
  other arithmetic  3.45 us (1%)
    unnamed x3, waiting for transfers between devices  137 us
    ppermute x12, waiting for transfers between devices, shift(): lax.ppermute(value, axis, [(i, (i + step) % size) for i in range(size)])  71.9 us
    ppermute x12, starting transfers between devices, shift(): lax.ppermute(value, axis, [(i, (i + step) % size) for i in range(size)])  33.2 us
    all_to_all x1, blocking collectives, shards(): lax.all_to_all(placed.reshape(experts, capacity, 2 * feat), 'expert', spl...  16.8 us
    all_to_all x1, starting transfers between devices, shards(): lax.all_to_all(payload, 'expert', split_axis=0, concat_axis=0, tiled=True)  13.4 us
    pallas_call x1, Pallas kernels, expert_part(): pl.pallas_call(functools.partial(expert_kernel, feat, ff, cap_rows, block...  12.3 us
  transfers between devices with their start and end apart: 15, of which 8 were waited for; matrix products, arithmetic and copies ran while one was open for 2% of the time, Pallas kernels for 0%

profile of v1, /device:TPU:1, one launch (start us, length us, event | category | flops | bytes accessed | tf_op | source)
XLA Modules:
  0.0 322.9 jit_solution(1081195995503045490)
XLA Ops:
  7.2 0.8 slice_bitcast_fusion.9
  8.1 0.2 select_reduce_fusion.1
  8.3 0.7 add_add_fusion
  9.0 1.1 convolution_convert_fusion
  10.2 16.8 %all_to_all.10 = bf16[8,36,512]{2,1,0:T(8,128)(2,1)S(1)} all-to-all(bf16[8,36,512]{2,1,0:T(8,128)(2,1)S(1)} %reshape.74), channel_id=1, replica_groups=mesh['expert'=8,'etensor'=16,'dp'=4] {'expert'}, dimensions={0} | all-to-all | bytes 589824 | tf_op jit(solution)/shard_map/all_to_all | solution.py:163
  26.9 0.8 all_gather_reshape.3
  27.8 1.9 collective-permute-start.4
  29.7 1.9 collective-permute-start.5
  31.7 3.4 %collective-permute-start = (bf16[1,1024,512]{2,1,0:T(8,128)(2,1)S(1)}, bf16[1,1024,512]{2,1,0:T(8,128)(2,1)S(1)}, u32[]{:S(2)}, u32[]{:S(2)}) collective-permute-start(bf16[1,1024,512]{2,1,0:T(8,128)(2,1)S(1)} %copy-done), channel_id=1, source_target_pairs={{0,1},{1,2},{2,3},{3,0},{4,5},{5,6},{6,7},{7,4},{8,9},{9,10},{10,1... | collective-permute-start | bytes 3145736 | tf_op jit(solution)/shard_map/ppermute | solution.py:128
  35.0 3.4 %collective-permute-start.1 = (bf16[1,1024,512]{2,1,0:T(8,128)(2,1)S(1)}, bf16[1,1024,512]{2,1,0:T(8,128)(2,1)S(1)}, u32[]{:S(2)}, u32[]{:S(2)}) collective-permute-start(bf16[1,1024,512]{2,1,0:T(8,128)(2,1)S(1)} %copy-done.1), channel_id=1, source_target_pairs={{0,1},{1,2},{2,3},{3,0},{4,5},{5,6},{6,7},{7,4},{8,9},{9,10},{10,1... | collective-permute-start | bytes 3145736 | tf_op jit(solution)/shard_map/ppermute | solution.py:128
  38.4 1.9 collective-permute-start.2
  40.3 13.4 %collective-permute-done.4.refs_7_ = bf16[1,1024,512]{2,1,0:T(8,128)(2,1)S(1)} collective-permute-done((bf16[1,1024,512]{2,1,0:T(8,128)(2,1)S(1)}, bf16[1,1024,512]{2,1,0:T(8,128)(2,1)S(1)}, u32[]{:S(2)}, u32[]{:S(2)}) %collective-permute-start.4) | collective-permute-done | bytes 1048608 | tf_op jit(solution)/shard_map/ppermute | solution.py:128
  53.7 3.4 %collective-permute-start.3 = (bf16[1,1024,512]{2,1,0:T(8,128)(2,1)S(1)}, bf16[1,1024,512]{2,1,0:T(8,128)(2,1)S(1)}, u32[]{:S(2)}, u32[]{:S(2)}) collective-permute-start(bf16[1,1024,512]{2,1,0:T(8,128)(2,1)S(1)} %copy-done), channel_id=1, source_target_pairs={{0,3},{1,0},{2,1},{3,2},{4,7},{5,4},{6,5},{7,6},{8,11},{9,8},{10,9... | collective-permute-start | bytes 3145736 | tf_op jit(solution)/shard_map/ppermute | solution.py:128
  57.2 18.9 %collective-permute-done.5.refs_8_ = bf16[1,512,1024]{2,1,0:T(8,128)(2,1)S(1)} collective-permute-done((bf16[1,512,1024]{2,1,0:T(8,128)(2,1)}, bf16[1,512,1024]{2,1,0:T(8,128)(2,1)S(1)}, u32[]{:S(2)}, u32[]{:S(2)}) %collective-permute-start.5) | collective-permute-done | bytes 1048608 | tf_op jit(solution)/shard_map/ppermute | solution.py:128
  76.1 3.5 %collective-permute-start.10 = (bf16[512,512]{1,0:T(8,128)(2,1)S(1)}, bf16[512,512]{1,0:T(8,128)(2,1)S(1)}, u32[]{:S(2)}, u32[]{:S(2)}) collective-permute-start(bf16[512,512]{1,0:T(8,128)(2,1)S(1)} %slice_bitcast_fusion.1), channel_id=1, source_target_pairs={{0,3},{1,0},{2,1},{3,2},{4,7},{5,4},{6,5},{7,6},{8,11},{9,8},{10,9... | collective-permute-start | bytes 1572872 | tf_op jit(solution)/shard_map/ppermute | solution.py:128
  79.7 0.8 slice_bitcast_fusion
  80.5 1.9 collective-permute-start.11
  82.4 0.9 slice_bitcast_fusion.5
  83.3 3.4 %collective-permute-start.6 = (bf16[512,512]{1,0:T(8,128)(2,1)}, bf16[512,512]{1,0:T(8,128)(2,1)}, u32[]{:S(2)}, u32[]{:S(2)}) collective-permute-start(bf16[512,512]{1,0:T(8,128)(2,1)} %slice_bitcast_fusion.5), channel_id=1, source_target_pairs={{0,1},{1,2},{2,3},{3,0},{4,5},{5,6},{6,7},{7,4},{8,9},{9,10},{10,1... | collective-permute-start | bytes 1572872 | tf_op jit(solution)/shard_map/ppermute | solution.py:128
  86.6 0.8 slice_bitcast_fusion.4
  87.5 16.1 %collective-permute-done.2.refs_5_ = bf16[1,512,1024]{2,1,0:T(8,128)(2,1)S(1)} collective-permute-done((bf16[1,512,1024]{2,1,0:T(8,128)(2,1)}, bf16[1,512,1024]{2,1,0:T(8,128)(2,1)S(1)}, u32[]{:S(2)}, u32[]{:S(2)}) %collective-permute-start.2) | collective-permute-done | bytes 1048608 | tf_op jit(solution)/shard_map/ppermute | solution.py:128
  103.6 2.0 collective-permute-start.7
  105.6 0.8 slice_bitcast_fusion.3
  106.4 3.1 collective-permute-start.8
  109.5 0.8 slice_bitcast_fusion.2
  110.4 3.4 %collective-permute-start.9 = (bf16[512,512]{1,0:T(8,128)(2,1)}, bf16[512,512]{1,0:T(8,128)(2,1)}, u32[]{:S(2)}, u32[]{:S(2)}) collective-permute-start(bf16[512,512]{1,0:T(8,128)(2,1)} %slice_bitcast_fusion.2), channel_id=1, source_target_pairs={{0,3},{1,0},{2,1},{3,2},{4,7},{5,4},{6,5},{7,6},{8,11},{9,8},{10,9... | collective-permute-start | bytes 1572872 | tf_op jit(solution)/shard_map/ppermute | solution.py:128
  113.9 7.2 %collective-permute-done.11.refs_14_ = bf16[256,1024]{1,0:T(8,128)(2,1)S(1)} collective-permute-done((bf16[256,1024]{1,0:T(8,128)(2,1)}, bf16[256,1024]{1,0:T(8,128)(2,1)S(1)}, u32[]{:S(2)}, u32[]{:S(2)}) %collective-permute-start.11) | collective-permute-done | bytes 524320 | tf_op jit(solution)/shard_map/ppermute | solution.py:128
  121.1 5.0 %collective-permute-done.7.refs_10_ = bf16[512,512]{1,0:T(8,128)(2,1)} collective-permute-done((bf16[512,512]{1,0:T(8,128)(2,1)}, bf16[512,512]{1,0:T(8,128)(2,1)}, u32[]{:S(2)}, u32[]{:S(2)}) %collective-permute-start.7) | collective-permute-done | bytes 524320 | tf_op jit(solution)/shard_map/ppermute | solution.py:128
  126.1 11.2 %collective-permute-done.8.refs_11_ = bf16[256,1024]{1,0:T(8,128)(2,1)} collective-permute-done((bf16[256,1024]{1,0:T(8,128)(2,1)}, bf16[256,1024]{1,0:T(8,128)(2,1)}, u32[]{:S(2)}, u32[]{:S(2)}) %collective-permute-start.8) | collective-permute-done | bytes 524320 | tf_op jit(solution)/shard_map/ppermute | solution.py:128
  137.4 12.3 %shard_map.86 = bf16[5104,256]{1,0:T(8,128)(2,1)} custom-call(s32[4]{0:T(128)S(1)} %pad_add_fusion.slot_of.order, s32[4]{0:T(128)S(1)} %pad_add_fusion.slot_of.order, s32[1]{0:T(128)} %bitcast.4.z_of, bf16[16,288,512]{2,1,0:T(8,128)(2,1)} %all-gather.2.cloned.1.call-done.recv, bf16[1,1024,512]{2,1,0:T(8,128)(2,1)S(1)} %copy-done, ...), custom_call_target="tpu_custom_call" | custom-call | flops 6039797760 | bytes 25165824 | tf_op jit(solution)/shard_map/pallas_call | solution.py:107
  149.7 1.3 dynamic-slice
  151.7 137.3 %all-reduce.3.cloned.1.call-done = bf16[5104,256]{1,0:T(8,128)(2,1)} async-done(((bf16[5104,256]{1,0:T(8,128)(2,1)}), bf16[5104,256]{1,0:T(8,128)(2,1)}) %all-reduce.3.cloned.1.call-update) | async-done | bytes 2613264
  289.0 0.7 dynamic-slice_convert_fusion
  289.8 1.0 constant_dynamic-slice_fusion
  290.9 0.1 concatenate.16
  291.0 0.8 maximum_maximum_fusion
  291.7 13.4 %all-to-all-start.1 = ((bf16[8,37,256]{2,1,0:T(8,128)(2,1)}), bf16[8,37,256]{2,1,0:T(8,128)(2,1)S(1)}, u32[]{:S(2)}, u32[]{:S(2)}) async-start(bf16[8,37,256]{2,1,0:T(8,128)(2,1)} %maximum_maximum_fusion), calls=%async_computation.1 | async-start | bytes 327680 | tf_op jit(solution)/shard_map/all_to_all | solution.py:192
  305.2 0.1 copy.13
  305.3 0.1 reshape.82
  305.4 0.1 copy.14
  305.5 5.2 %all-to-all-done.1 = bf16[8,37,256]{2,1,0:T(8,128)(2,1)S(1)} async-done(((bf16[8,37,256]{2,1,0:T(8,128)(2,1)}), bf16[8,37,256]{2,1,0:T(8,128)(2,1)S(1)}, u32[]{:S(2)}, u32[]{:S(2)}) %all-to-all-start.1) | async-done | bytes 151584 | tf_op jit(solution)/shard_map/all_to_all | solution.py:192
  310.8 1.2 gather_fusion
  311.9 0.1 reshape.79
  312.1 0.1 fusion.13
  312.2 1.9 gather_fusion.1
  314.2 0.1 reshape.78
  314.3 0.6 copy.15
  315.0 1.0 multiply_reduce_fusion
  (46 shorter events, 0.7 us)
Async XLA Ops:
  7.2 20.6 %copy-start.1 = (bf16[1,1024,512]{2,1,0:T(8,128)(2,1)S(1)}, bf16[1,1024,512]{2,1,0:T(8,128)(2,1)}, u32[]{:S(2)}) copy-start(bf16[1,1024,512]{2,1,0:T(8,128)(2,1)} %refs_1_.1) | copy-start | bytes 3145732
  7.2 24.5 %copy-start = (bf16[1,1024,512]{2,1,0:T(8,128)(2,1)S(1)}, bf16[1,1024,512]{2,1,0:T(8,128)(2,1)}, u32[]{:S(2)}) copy-start(bf16[1,1024,512]{2,1,0:T(8,128)(2,1)} %refs_0_.1) | copy-start | bytes 3145732
  7.2 130.2 %all-gather.2.cloned.1.call-start = ((), (), s32[]{:S(2)}) async-start(), calls=%async_computation.2 | async-start | bytes 5013504 | tf_op jit(solution)/shard_map/all_gather | solution.py:166
  27.7 261.3 %all-reduce.3.cloned.1.call-start = ((), (), s32[]{:S(2)}) async-start(), calls=%async_computation.3 | async-start | bytes 5226496
  27.8 25.9 %collective-permute-start.4 = (bf16[1,1024,512]{2,1,0:T(8,128)(2,1)S(1)}, bf16[1,1024,512]{2,1,0:T(8,128)(2,1)S(1)}, u32[]{:S(2)}, u32[]{:S(2)}) collective-permute-start(bf16[1,1024,512]{2,1,0:T(8,128)(2,1)S(1)} %copy-done.1), channel_id=1, source_target_pairs={{0,3},{1,0},{2,1},{3,2},{4,7},{5,4},{6,5},{7,6},{8,11},{9,8},{10,9... | collective-permute-start | bytes 3145736 | tf_op jit(solution)/shard_map/ppermute | solution.py:128
  29.7 46.4 %collective-permute-start.5 = (bf16[1,512,1024]{2,1,0:T(8,128)(2,1)}, bf16[1,512,1024]{2,1,0:T(8,128)(2,1)S(1)}, u32[]{:S(2)}, u32[]{:S(2)}) collective-permute-start(bf16[1,512,1024]{2,1,0:T(8,128)(2,1)} %refs_2_.1), channel_id=1, source_target_pairs={{0,3},{1,0},{2,1},{3,2},{4,7},{5,4},{6,5},{7,6},{8,11},{9,8},{10,9... | collective-permute-start | bytes 3145736 | tf_op jit(solution)/shard_map/ppermute | solution.py:128
  31.7 48.8 %collective-permute-start = (bf16[1,1024,512]{2,1,0:T(8,128)(2,1)S(1)}, bf16[1,1024,512]{2,1,0:T(8,128)(2,1)S(1)}, u32[]{:S(2)}, u32[]{:S(2)}) collective-permute-start(bf16[1,1024,512]{2,1,0:T(8,128)(2,1)S(1)} %copy-done), channel_id=1, source_target_pairs={{0,1},{1,2},{2,3},{3,0},{4,5},{5,6},{6,7},{7,4},{8,9},{9,10},{10,1... | collective-permute-start | bytes 3145736 | tf_op jit(solution)/shard_map/ppermute | solution.py:128
  35.0 48.3 %collective-permute-start.1 = (bf16[1,1024,512]{2,1,0:T(8,128)(2,1)S(1)}, bf16[1,1024,512]{2,1,0:T(8,128)(2,1)S(1)}, u32[]{:S(2)}, u32[]{:S(2)}) collective-permute-start(bf16[1,1024,512]{2,1,0:T(8,128)(2,1)S(1)} %copy-done.1), channel_id=1, source_target_pairs={{0,1},{1,2},{2,3},{3,0},{4,5},{5,6},{6,7},{7,4},{8,9},{9,10},{10,1... | collective-permute-start | bytes 3145736 | tf_op jit(solution)/shard_map/ppermute | solution.py:128
  38.4 65.2 %collective-permute-start.2 = (bf16[1,512,1024]{2,1,0:T(8,128)(2,1)}, bf16[1,512,1024]{2,1,0:T(8,128)(2,1)S(1)}, u32[]{:S(2)}, u32[]{:S(2)}) collective-permute-start(bf16[1,512,1024]{2,1,0:T(8,128)(2,1)} %refs_2_.1), channel_id=1, source_target_pairs={{0,1},{1,2},{2,3},{3,0},{4,5},{5,6},{6,7},{7,4},{8,9},{9,10},{10,1... | collective-permute-start | bytes 3145736 | tf_op jit(solution)/shard_map/ppermute | solution.py:128
  53.7 52.7 %copy-start.2 = (bf16[1,1024,512]{2,1,0:T(8,128)(2,1)}, bf16[1,1024,512]{2,1,0:T(8,128)(2,1)S(1)}, u32[]{:S(2)}) copy-start(bf16[1,1024,512]{2,1,0:T(8,128)(2,1)S(1)} %collective-permute-done.4.refs_7_) | copy-start | bytes 3145732
  53.7 52.7 %collective-permute-start.3 = (bf16[1,1024,512]{2,1,0:T(8,128)(2,1)S(1)}, bf16[1,1024,512]{2,1,0:T(8,128)(2,1)S(1)}, u32[]{:S(2)}, u32[]{:S(2)}) collective-permute-start(bf16[1,1024,512]{2,1,0:T(8,128)(2,1)S(1)} %copy-done), channel_id=1, source_target_pairs={{0,3},{1,0},{2,1},{3,2},{4,7},{5,4},{6,5},{7,6},{8,11},{9,8},{10,9... | collective-permute-start | bytes 3145736 | tf_op jit(solution)/shard_map/ppermute | solution.py:128
  76.1 34.2 %copy-start.3 = (bf16[1,512,1024]{2,1,0:T(8,128)(2,1)}, bf16[1,512,1024]{2,1,0:T(8,128)(2,1)S(1)}, u32[]{:S(2)}) copy-start(bf16[1,512,1024]{2,1,0:T(8,128)(2,1)S(1)} %collective-permute-done.5.refs_8_) | copy-start | bytes 3145732
  76.1 34.2 %collective-permute-start.10 = (bf16[512,512]{1,0:T(8,128)(2,1)S(1)}, bf16[512,512]{1,0:T(8,128)(2,1)S(1)}, u32[]{:S(2)}, u32[]{:S(2)}) collective-permute-start(bf16[512,512]{1,0:T(8,128)(2,1)S(1)} %slice_bitcast_fusion.1), channel_id=1, source_target_pairs={{0,3},{1,0},{2,1},{3,2},{4,7},{5,4},{6,5},{7,6},{8,11},{9,8},{10,9... | collective-permute-start | bytes 1572872 | tf_op jit(solution)/shard_map/ppermute | solution.py:128
  80.5 29.9 %copy-start.4 = (bf16[1,1024,512]{2,1,0:T(8,128)(2,1)}, bf16[1,1024,512]{2,1,0:T(8,128)(2,1)S(1)}, u32[]{:S(2)}) copy-start(bf16[1,1024,512]{2,1,0:T(8,128)(2,1)S(1)} %collective-permute-done.refs_3_) | copy-start | bytes 3145732
  80.5 40.7 %collective-permute-start.11 = (bf16[256,1024]{1,0:T(8,128)(2,1)}, bf16[256,1024]{1,0:T(8,128)(2,1)S(1)}, u32[]{:S(2)}, u32[]{:S(2)}) collective-permute-start(bf16[256,1024]{1,0:T(8,128)(2,1)} %slice_bitcast_fusion), channel_id=1, source_target_pairs={{0,3},{1,0},{2,1},{3,2},{4,7},{5,4},{6,5},{7,6},{8,11},{9,8},{10,9... | collective-permute-start | bytes 1572872 | tf_op jit(solution)/shard_map/ppermute | solution.py:128
  83.3 30.5 %copy-start.5 = (bf16[1,1024,512]{2,1,0:T(8,128)(2,1)}, bf16[1,1024,512]{2,1,0:T(8,128)(2,1)S(1)}, u32[]{:S(2)}) copy-start(bf16[1,1024,512]{2,1,0:T(8,128)(2,1)S(1)} %collective-permute-done.1.refs_4_) | copy-start | bytes 3145732
  83.3 37.9 %collective-permute-start.6 = (bf16[512,512]{1,0:T(8,128)(2,1)}, bf16[512,512]{1,0:T(8,128)(2,1)}, u32[]{:S(2)}, u32[]{:S(2)}) collective-permute-start(bf16[512,512]{1,0:T(8,128)(2,1)} %slice_bitcast_fusion.5), channel_id=1, source_target_pairs={{0,1},{1,2},{2,3},{3,0},{4,5},{5,6},{6,7},{7,4},{8,9},{9,10},{10,1... | collective-permute-start | bytes 1572872 | tf_op jit(solution)/shard_map/ppermute | solution.py:128
  103.6 10.2 %copy-start.6 = (bf16[1,512,1024]{2,1,0:T(8,128)(2,1)}, bf16[1,512,1024]{2,1,0:T(8,128)(2,1)S(1)}, u32[]{:S(2)}) copy-start(bf16[1,512,1024]{2,1,0:T(8,128)(2,1)S(1)} %collective-permute-done.2.refs_5_) | copy-start | bytes 3145732
  103.6 22.6 %collective-permute-start.7 = (bf16[512,512]{1,0:T(8,128)(2,1)}, bf16[512,512]{1,0:T(8,128)(2,1)}, u32[]{:S(2)}, u32[]{:S(2)}) collective-permute-start(bf16[512,512]{1,0:T(8,128)(2,1)} %slice_bitcast_fusion.4), channel_id=1, source_target_pairs={{0,1},{1,2},{2,3},{3,0},{4,5},{5,6},{6,7},{7,4},{8,9},{9,10},{10,1... | collective-permute-start | bytes 1572872 | tf_op jit(solution)/shard_map/ppermute | solution.py:128
  106.4 7.4 %copy-start.7 = (bf16[1,1024,512]{2,1,0:T(8,128)(2,1)}, bf16[1,1024,512]{2,1,0:T(8,128)(2,1)S(1)}, u32[]{:S(2)}) copy-start(bf16[1,1024,512]{2,1,0:T(8,128)(2,1)S(1)} %collective-permute-done.3.refs_6_) | copy-start | bytes 3145732
  106.4 30.9 %collective-permute-start.8 = (bf16[256,1024]{1,0:T(8,128)(2,1)}, bf16[256,1024]{1,0:T(8,128)(2,1)}, u32[]{:S(2)}, u32[]{:S(2)}) collective-permute-start(bf16[256,1024]{1,0:T(8,128)(2,1)} %slice_bitcast_fusion.3), channel_id=1, source_target_pairs={{0,1},{1,2},{2,3},{3,0},{4,5},{5,6},{6,7},{7,4},{8,9},{9,10},{10,1... | collective-permute-start | bytes 1572872 | tf_op jit(solution)/shard_map/ppermute | solution.py:128
  110.4 27.0 %collective-permute-start.9 = (bf16[512,512]{1,0:T(8,128)(2,1)}, bf16[512,512]{1,0:T(8,128)(2,1)}, u32[]{:S(2)}, u32[]{:S(2)}) collective-permute-start(bf16[512,512]{1,0:T(8,128)(2,1)} %slice_bitcast_fusion.2), channel_id=1, source_target_pairs={{0,3},{1,0},{2,1},{3,2},{4,7},{5,4},{6,5},{7,6},{8,11},{9,8},{10,9... | collective-permute-start | bytes 1572872 | tf_op jit(solution)/shard_map/ppermute | solution.py:128
  149.6 155.8 %copy-start.8 = (f32[128,2]{0,1:T(2,128)S(1)}, f32[128,2]{0,1:T(2,128)}, u32[]{:S(2)}) copy-start(f32[128,2]{0,1:T(2,128)} %param.10) | copy-start | bytes 3076
  291.7 19.0 %all-to-all-start.1 = ((bf16[8,37,256]{2,1,0:T(8,128)(2,1)}), bf16[8,37,256]{2,1,0:T(8,128)(2,1)S(1)}, u32[]{:S(2)}, u32[]{:S(2)}) async-start(bf16[8,37,256]{2,1,0:T(8,128)(2,1)} %maximum_maximum_fusion), calls=%async_computation.1 | async-start | bytes 327680 | tf_op jit(solution)/shard_map/all_to_all | solution.py:192
Sparse Core Ops, SparseCore 0:
  27.8 71.3 all-gather.1
  149.8 139.1 all-reduce.2

commit v2 on v1

v2 whole, which is shorter than its diff:
```python
import functools

import jax
import jax.numpy as jnp
from jax import lax
from jax.experimental import pallas as pl
from jax.experimental.pallas import tpu as pltpu
from jax.sharding import PartitionSpec as P

NT = (((1,), (1,)), ((), ()))


HBM = pl.BlockSpec(memory_space=pltpu.HBM)
VMEM = pl.BlockSpec(memory_space=pltpu.VMEM)
SMEM = pl.BlockSpec(memory_space=pltpu.SMEM)


def fetch(src, dst, sem):
    copy = pltpu.make_async_copy(src, dst, sem)
    copy.start()
    copy.wait()


STEPS = (64, 32, 16, 8, 4, 2, 1)


def code_kernel(rows_hbm, coded, rows, sem):
    fetch(rows_hbm, rows, sem)
    owners, capacity, both = rows.shape
    feat = both // 2
    values = jnp.concatenate([rows[e].astype(jnp.float32) for e in range(owners)], axis=0)
    largest = jnp.max(jnp.abs(values), axis=0, keepdims=True)
    largest = jnp.concatenate(
        [
            jnp.broadcast_to(jnp.max(half, axis=1, keepdims=True), (1, feat))
            for half in (largest[:, :feat], largest[:, feat:])
        ],
        axis=1,
    )
    scale = jnp.ones((1, both), jnp.float32)
    power = jnp.zeros((1, both), jnp.int32)
    for step in STEPS:
        fits = largest * (2.0**step) <= 32000.0
        largest = jnp.where(fits, largest * (2.0**step), largest)
        scale = jnp.where(fits, scale * (2.0**step), scale)
        power = jnp.where(fits, power + step, power)
    whole = jnp.round(values * scale).astype(jnp.int32)
    tail = jnp.broadcast_to(power, (coded.shape[0] - owners * capacity, both))
    coded[...] = jnp.concatenate([whole, tail], axis=0).astype(jnp.int16)


def code(rows, lines):
    owners, capacity, both = rows.shape
    return pl.pallas_call(
        code_kernel,
        out_shape=jax.ShapeDtypeStruct((lines, both), jnp.int16),
        in_specs=[HBM],
        out_specs=VMEM,
        scratch_shapes=[pltpu.VMEM(rows.shape, rows.dtype), pltpu.SemaphoreType.DMA(())],
        compiler_params=pltpu.CompilerParams(vmem_limit_bytes=8 << 20),
    )(rows)


def decode(block, cap_rows):
    power = block[cap_rows:].astype(jnp.int32)[0:1]
    scale = jnp.ones(power.shape, jnp.float32)
    for step in STEPS:
        taken = power >= step
        scale = jnp.where(taken, scale * (0.5**step), scale)
        power = jnp.where(taken, power - step, power)
    return (block[:cap_rows].astype(jnp.int32).astype(jnp.float32) * scale).astype(jnp.bfloat16)


def back_kernel(cap_rows, coded, down, parts, coded_v, down_v, parts_v, sems):
    groups = parts.shape[0]
    per = coded.shape[0] // groups
    feat = coded.shape[2] // 2
    weight = pltpu.make_async_copy(down.at[0], down_v, sems.at[groups])
    weight.start()
    copies = [
        pltpu.make_async_copy(
            coded.at[pl.ds(per * g, per), :, pl.ds(feat, feat)], coded_v.at[g], sems.at[g]
        )
        for g in range(groups)
    ]
    for copy in copies:
        copy.start()
    weight.wait()
    sent = []
    for g in range(groups):
        copies[g].wait()
        y = jnp.concatenate([decode(coded_v[g, k], cap_rows) for k in range(per)], axis=1)
        parts_v[g] = lax.dot_general(y, down_v[...], NT, preferred_element_type=jnp.float32).astype(
            jnp.bfloat16
        )
        sent.append(pltpu.make_async_copy(parts_v.at[g], parts.at[g], sems.at[groups + 1 + g]))
        sent[g].start()
    for copy in sent:
        copy.wait()


def back_parts(coded, down, cap_rows, groups):
    blocks, lines, both = coded.shape
    _, ff, depth = down.shape
    return pl.pallas_call(
        functools.partial(back_kernel, cap_rows),
        out_shape=pltpu.HBM((groups, cap_rows, ff), jnp.bfloat16),
        in_specs=[HBM, HBM],
        out_specs=HBM,
        scratch_shapes=[
            pltpu.VMEM((groups, blocks // groups, lines, both // 2), jnp.int16),
            pltpu.VMEM((ff, depth), jnp.bfloat16),
            pltpu.VMEM((groups, cap_rows, ff), jnp.bfloat16),
            pltpu.SemaphoreType.DMA((2 * groups + 1,)),
        ],
        compiler_params=pltpu.CompilerParams(vmem_limit_bytes=24 << 20),
        cost_estimate=pl.CostEstimate(
            flops=2 * groups * cap_rows * depth * ff, bytes_accessed=5 << 20, transcendentals=0
        ),
    )(coded, down)


def hidden_kernel(cap_rows, slot_of, coded, *refs):
    weights, (gate_out, up_out, gate_pre, up_pre, rows_v, w_v, sems) = refs[:4], refs[4:]
    per = coded.shape[0] // 4
    feat = coded.shape[2] // 2
    waits = []
    for s in range(4):
        rows = coded.at[pl.ds(slot_of[s] * per, per), :, pl.ds(0, feat)]
        waits.append(
            [
                pltpu.make_async_copy(rows, rows_v.at[s], sems.at[2 * s]),
                pltpu.make_async_copy(weights[s], w_v.at[s], sems.at[2 * s + 1]),
            ]
        )
        for copy in waits[s]:
            copy.start()
    for s in range(4):
        for copy in waits[s]:
            copy.wait()
        x = jnp.concatenate([decode(rows_v[s, k], cap_rows) for k in range(per)], axis=1)
        g = jnp.dot(x, w_v[s, 0], preferred_element_type=jnp.float32)
        u = jnp.dot(x, w_v[s, 1], preferred_element_type=jnp.float32)
        if s == 0:
            gate_pre[...], up_pre[...] = g, u
        else:
            gate_pre[...] += g
            up_pre[...] += u
    sent = [
        pltpu.make_async_copy(gate_pre, gate_out, sems.at[8]),
        pltpu.make_async_copy(up_pre, up_out, sems.at[9]),
    ]
    for copy in sent:
        copy.start()
    for copy in sent:
        copy.wait()


def hidden_part(coded, weights, slot_of, cap_rows):
    blocks, lines, both = coded.shape
    _, depth, ff = weights[0].shape
    result = pltpu.HBM((cap_rows, ff), jnp.float32)
    return pl.pallas_call(
        functools.partial(hidden_kernel, cap_rows),
        out_shape=(result, result),
        in_specs=[SMEM] + [HBM] * 5,
        out_specs=(HBM, HBM),
        scratch_shapes=[
            pltpu.VMEM((cap_rows, ff), jnp.float32),
            pltpu.VMEM((cap_rows, ff), jnp.float32),
            pltpu.VMEM((4, blocks // 4, lines, both // 2), jnp.int16),
            pltpu.VMEM((4, 2, depth, ff), jnp.bfloat16),
            pltpu.SemaphoreType.DMA((10,)),
        ],
        compiler_params=pltpu.CompilerParams(vmem_limit_bytes=32 << 20),
        cost_estimate=pl.CostEstimate(
            flops=4 * cap_rows * 4 * depth * ff, bytes_accessed=12 << 20, transcendentals=0
        ),
    )(slot_of, coded, *weights)


def term_kernel(pitch, slots, slot_of, z_of, gate_hbm, up_hbm, backs_hbm, *refs):
    weights, (out, gate_ref, up_ref, backs, w_v, out_v, blank, sems) = refs[:4], refs[4:]
    cap_rows = gate_ref.shape[0]
    feat = out.shape[1]
    per = w_v.shape[2] // feat
    first = [
        pltpu.make_async_copy(src, dst, sems.at[4 + i])
        for i, (src, dst) in enumerate(((gate_hbm, gate_ref), (up_hbm, up_ref), (backs_hbm, backs)))
    ]
    for copy in first:
        copy.start()
    waits = [pltpu.make_async_copy(weights[s], w_v.at[s], sems.at[s]) for s in range(4)]
    for copy in waits:
        copy.start()
    for copy in first:
        copy.wait()
    gate_pre, up_pre = gate_ref[...], up_ref[...]
    for s in range(4):
        b = backs[s].astype(jnp.float32)
        back = b if s == 0 else back + b
    sig = 1.0 / (1.0 + jnp.exp(-gate_pre))
    act = gate_pre * sig
    prod = act * up_pre * back
    d_gate = (back * up_pre * sig * (1.0 + gate_pre * (1.0 - sig))).astype(jnp.bfloat16)
    d_up = (back * act).astype(jnp.bfloat16)

    ones = jnp.ones((16, prod.shape[1]), jnp.bfloat16)
    total = None
    rest = prod
    for _ in range(3):
        limb = rest.astype(jnp.bfloat16)
        rest = rest - limb.astype(jnp.float32)
        part = lax.dot_general(ones, limb, NT, preferred_element_type=jnp.float32)
        total = part if total is None else total + part
    top = total.astype(jnp.bfloat16).astype(jnp.float32)
    low = total - top
    over = cap_rows - feat
    row = lax.broadcasted_iota(jnp.int32, (16, feat), 0)
    lane = lax.broadcasted_iota(jnp.int32, (16, feat), 1)
    q = z_of[0]
    mine = (lane >= q * over) & (lane < (q + 1) * over)
    wide = lambda v: jnp.concatenate([v[:, feat:]] * (feat // over), axis=1)
    extra = jnp.where(row == q, top[:, :feat], 0.0)
    extra = jnp.where(row == q + slots, low[:, :feat], extra)
    extra = jnp.where((row == 2 * slots) & mine, wide(top), extra)
    extra = jnp.where((row == 2 * slots + 1) & mine, wide(low), extra)
    extra = extra.astype(jnp.bfloat16)
    tail = pitch - cap_rows - 16
    span = per * pitch - tail
    blank[...] = jnp.zeros(blank.shape, blank.dtype)
    sent = []
    for j in range(3):
        sent.append(
            pltpu.make_async_copy(
                blank, out.at[pl.ds(j * per * pitch + span, tail)], sems.at[11 + j]
            )
        )
        sent[j].start()
    for s in range(4):
        waits[s].wait()
        term = lax.dot_general(d_gate, w_v[s, 0], NT, preferred_element_type=jnp.float32)
        term = term + lax.dot_general(d_up, w_v[s, 1], NT, preferred_element_type=jnp.float32)
        for k in range(per):
            at = k * pitch
            out_v[s, at : at + cap_rows] = term[:, k * feat : (k + 1) * feat].astype(jnp.bfloat16)
            out_v[s, at + cap_rows : at + cap_rows + 16] = extra
            if k + 1 < per:
                out_v[s, at + cap_rows + 16 : at + pitch] = jnp.zeros((tail, feat), jnp.bfloat16)
        at = pl.multiple_of(slot_of[s] * (per * pitch), 16)
        sent.append(pltpu.make_async_copy(out_v.at[s], out.at[pl.ds(at, span)], sems.at[7 + s]))
        sent[3 + s].start()
    for copy in sent:
        copy.wait()


def term_part(gate_pre, up_pre, backs, weights, slot_of, z_index, feat, pitch, out_rows, slots):
    cap_rows, ff = gate_pre.shape
    depth = weights[0].shape[1]
    z_of = jnp.reshape(z_index % slots, (1,)).astype(jnp.int32)
    per = depth // feat
    return pl.pallas_call(
        functools.partial(term_kernel, pitch, slots),
        out_shape=pltpu.HBM((out_rows, feat), jnp.bfloat16),
        in_specs=[SMEM, SMEM] + [HBM] * 7,
        out_specs=HBM,
        scratch_shapes=[
            pltpu.VMEM((cap_rows, ff), jnp.float32),
            pltpu.VMEM((cap_rows, ff), jnp.float32),
            pltpu.VMEM((4, cap_rows, ff), jnp.bfloat16),
            pltpu.VMEM((4, 2, depth, ff), jnp.bfloat16),
            pltpu.VMEM((4, per * pitch - 16, feat), jnp.bfloat16),
            pltpu.VMEM((16, feat), jnp.bfloat16),
            pltpu.SemaphoreType.DMA((14,)),
        ],
        compiler_params=pltpu.CompilerParams(vmem_limit_bytes=40 << 20),
        cost_estimate=pl.CostEstimate(
            flops=4 * cap_rows * 4 * depth * ff, bytes_accessed=14 << 20, transcendentals=cap_rows * ff
        ),
    )(slot_of, z_of, gate_pre, up_pre, backs, *weights)


def place_kernel(capacity, routes, tokens, moved_hbm, placed, slot, moved, sem):
    fetch(moved_hbm, moved, sem)
    tok_rows, feat = tokens.shape
    experts = placed.shape[0]
    ids = lax.broadcasted_iota(jnp.int32, (16, tok_rows), 0)
    place_of = lax.broadcasted_iota(jnp.int32, (48, tok_rows), 0)
    before = lax.broadcasted_iota(jnp.int32, (tok_rows, tok_rows), 0) < lax.broadcasted_iota(
        jnp.int32, (tok_rows, tok_rows), 1
    )
    as_ones = lambda mask: jnp.where(mask, 1.0, 0.0).astype(jnp.bfloat16)

    def slots_of(first, second):
        hot = (first == ids) | (second == ids)
        ranks = jnp.dot(as_ones(hot), as_ones(before), preferred_element_type=jnp.float32)
        return [
            jnp.sum(jnp.where(r == ids, ranks, 0.0), axis=0, keepdims=True).astype(jnp.int32)
            for r in (first, second)
        ]

    far = moved[tok_rows:].astype(jnp.float32).astype(jnp.int32)
    kinds = []
    for first, second, rows in (
        (routes[0:1, :], routes[1:2, :], tokens[...]),
        (far[0:1, :tok_rows], far[1:2, :tok_rows], moved[:tok_rows]),
    ):
        kinds.append((first, second, slots_of(first, second), rows))
    slot[...] = jnp.concatenate(kinds[0][2], axis=0)
    for e in range(experts):
        found = []
        for first, second, slots, rows in kinds:
            wanted = jnp.where(first == e, slots[0], jnp.where(second == e, slots[1], -1))
            found.append(
                jnp.dot(as_ones(wanted == place_of), rows, preferred_element_type=jnp.float32)
            )
        placed[e] = jnp.concatenate(found, axis=1)[:capacity].astype(jnp.bfloat16)


def place(routes, tokens, moved, experts, capacity):
    tok_rows, feat = tokens.shape
    vmem = pl.BlockSpec(memory_space=pltpu.VMEM)
    return pl.pallas_call(
        functools.partial(place_kernel, capacity),
        out_shape=(
            jax.ShapeDtypeStruct((experts, capacity, 2 * feat), jnp.bfloat16),
            jax.ShapeDtypeStruct((2, tok_rows), jnp.int32),
        ),
        in_specs=[vmem, vmem, HBM],
        out_specs=(vmem, vmem),
        scratch_shapes=[pltpu.VMEM(moved.shape, moved.dtype), pltpu.SemaphoreType.DMA(())],
        compiler_params=pltpu.CompilerParams(vmem_limit_bytes=8 << 20),
    )(routes, tokens, moved)


def pack_kernel(owners, capacity, slots, z_of, summed, payload, wide):
    feat = summed.shape[1]
    cap_rows = owners * capacity
    over = cap_rows - feat
    count = wide.shape[0]
    wide[pl.ds(0, summed.shape[0]), :] = summed[...].astype(jnp.float32)
    lined = pltpu.roll(wide[...], lax.rem(count - z_of[0], count), 0)
    extra = lined[cap_rows : cap_rows + 16]
    row = lax.broadcasted_iota(jnp.int32, (16, feat), 0)
    lane = lax.broadcasted_iota(jnp.int32, (16, feat), 1)
    head = jnp.sum(jnp.where(row < 2 * slots, extra, 0.0), axis=0, keepdims=True)
    tail = jnp.sum(
        jnp.where((row >= 2 * slots) & (lane < slots * over), extra, 0.0), axis=0, keepdims=True
    )
    tail = sum(tail[:, over * q : over * (q + 1)] for q in range(slots))
    gates = jnp.concatenate([head, tail], axis=1)
    top = gates.astype(jnp.bfloat16).astype(jnp.float32)
    low = gates - top
    blank = jnp.zeros((1, feat - 2 * capacity), jnp.float32)
    rest = jnp.zeros((payload.shape[1] - capacity - 1, feat), jnp.float32)
    for d in range(owners):
        cut = slice(capacity * d, capacity * (d + 1))
        line = jnp.concatenate([top[:, cut], low[:, cut], blank], axis=1)
        rows = lined[capacity * d : capacity * (d + 1)]
        payload[d] = jnp.concatenate([rows, line, rest], axis=0).astype(jnp.bfloat16)


def pack(summed, z_index, owners, capacity, slots, lines):
    rows, feat = summed.shape
    vmem = pl.BlockSpec(memory_space=pltpu.VMEM)
    return pl.pallas_call(
        functools.partial(pack_kernel, owners, capacity, slots),
        out_shape=jax.ShapeDtypeStruct((owners, lines, feat), jnp.bfloat16),
        in_specs=[pl.BlockSpec(memory_space=pltpu.SMEM), vmem],
        out_specs=vmem,
        scratch_shapes=[pltpu.VMEM((rows + 1, feat), jnp.float32)],
    )(jnp.reshape(z_index, (1,)).astype(jnp.int32), summed)


def combine_kernel(capacity, routes, slot, probs, came_hbm, input_grad, gate_grad, came, sem):
    fetch(came_hbm, came, sem)
    tok_rows = routes.shape[1]
    experts, lines, feat = came.shape
    flat = came[...].reshape(experts * lines, feat)
    place_of = lax.broadcasted_iota(jnp.int32, (experts * lines, tok_rows), 0)
    weight = jnp.zeros(place_of.shape, jnp.float32)
    for k in range(2):
        at = routes[k : k + 1, :] * lines + slot[k : k + 1, :]
        weight = jnp.where(place_of == at, probs[k : k + 1, :], weight)
    total = None
    for _ in range(3):
        limb = weight.astype(jnp.bfloat16)
        weight = weight - limb.astype(jnp.float32)
        part = lax.dot_general(
            limb, flat, (((0,), (0,)), ((), ())), preferred_element_type=jnp.float32
        )
        total = part if total is None else total + part
    input_grad[...] = total.astype(jnp.bfloat16)

    gates = jnp.concatenate(
        [came[e, 32:48].astype(jnp.float32)[capacity - 32 : capacity - 31] for e in range(experts)], axis=0
    ).astype(jnp.bfloat16)
    lane_of = lax.broadcasted_iota(jnp.int32, (feat, tok_rows), 0)
    ids = lax.broadcasted_iota(jnp.int32, (experts, tok_rows), 0)
    lines_of = []
    for k in range(2):
        s = slot[k : k + 1, :]
        pick = jnp.where((lane_of == s) | (lane_of == s + capacity), 1.0, 0.0).astype(jnp.bfloat16)
        values = jnp.dot(gates, pick, preferred_element_type=jnp.float32)
        lines_of.append(
            jnp.sum(jnp.where(routes[k : k + 1, :] == ids, values, 0.0), axis=0, keepdims=True)
        )
    gate_grad[...] = jnp.concatenate(lines_of, axis=0)


def combine(routes, slot, probs, came, capacity):
    tok_rows = routes.shape[1]
    feat = came.shape[2]
    vmem = pl.BlockSpec(memory_space=pltpu.VMEM)
    return pl.pallas_call(
        functools.partial(combine_kernel, capacity),
        out_shape=(
            jax.ShapeDtypeStruct((tok_rows, feat), jnp.bfloat16),
            jax.ShapeDtypeStruct((2, tok_rows), jnp.float32),
        ),
        in_specs=[vmem] * 3 + [HBM],
        out_specs=(vmem, vmem),
        scratch_shapes=[pltpu.VMEM(came.shape, came.dtype), pltpu.SemaphoreType.DMA(())],
        compiler_params=pltpu.CompilerParams(vmem_limit_bytes=8 << 20),
    )(routes, slot, probs, came)


def shift(value, axis, step):
    size = lax.axis_size(axis)
    return lax.ppermute(value, axis, [(i, (i + step) % size) for i in range(size)])


def shards(tokens, out_grad, routes, gate_probs, gate_weight, up_weight, down_weight):
    tok_rows, feat = tokens.shape
    owners = lax.axis_size("expert")
    blocks = lax.axis_size("etensor")
    experts = owners * gate_weight.shape[0]
    capacity = min(tok_rows, 9 * tok_rows // (4 * experts))
    x_index = lax.axis_index("dp")
    z_index = lax.axis_index("etensor")
    cap_rows = owners * capacity
    slots = 7

    columns = lax.axis_size("dp")
    gate_up = jnp.concatenate([gate_weight, up_weight], axis=0)

    per = blocks // columns
    swap = [
        ((columns * a + w) * columns + x, (columns * x + w) * columns + a)
        for a in range(columns)
        for w in range(per)
        for x in range(columns)
    ]
    tags = jnp.pad(routes.T.astype(jnp.bfloat16), ((0, 14), (0, feat - tok_rows)))
    moved = lax.ppermute(jnp.concatenate([out_grad, tags], axis=0), ("etensor", "dp"), swap)

    def send():
        placed, slot = place(routes.T, tokens, moved, experts, capacity)
        part = lax.all_to_all(placed, "expert", split_axis=0, concat_axis=0, tiled=True)
        return code(part, cap_rows + 16), slot

    coded, slot = lax.cond(
        routes[0, 0] >= 0,
        send,
        lambda: (
            jnp.zeros((cap_rows + 16, 2 * feat), jnp.int16),
            jnp.zeros((2, tok_rows), jnp.int32),
        ),
    )
    coded = lax.all_gather(coded, "etensor", axis=0, tiled=False)
    coded = pltpu.with_memory_space_constraint(coded, pltpu.HBM)
    backs = lax.all_to_all(
        back_parts(coded, down_weight, cap_rows, columns), "dp", split_axis=0, concat_axis=0, tiled=True
    )

    weights = (gate_up,) + tuple(shift(gate_up, "dp", step) for step in (1, -1, 2))
    slot_of = jnp.stack([(x_index + step) % 4 for step in (0, 3, 1, 2)]).astype(jnp.int32)
    gate_pre, up_pre = (
        pltpu.with_memory_space_constraint(v, pltpu.HBM)
        for v in hidden_part(coded, weights, slot_of, cap_rows)
    )
    pitch = cap_rows + 32
    terms = term_part(
        gate_pre, up_pre, backs, weights, slot_of, z_index, feat, pitch, blocks * (pitch - 1), slots
    )
    summed = lax.psum_scatter(terms, "etensor", scatter_dimension=0, tiled=True)
    payload = pack(summed, z_index, owners, capacity, slots, 48)
    came = lax.all_to_all(payload, "expert", split_axis=0, concat_axis=0, tiled=True)
    input_grad, gate_grad = combine(routes.T, slot, gate_probs.T, came, capacity)
    return input_grad, gate_grad.T


def solution(mesh):
    return jax.shard_map(
        shards,
        mesh=mesh,
        in_specs=(
            P(("expert", "dp"), "etensor"),
            P(("expert", "dp"), "etensor"),
            P(("expert", "dp"), None),
            P(("expert", "dp"), None),
            P("expert", "dp", "etensor"),
            P("expert", "dp", "etensor"),
            P("expert", "etensor", "dp"),
        ),
        out_specs=(P(("expert", "dp"), "etensor"), P(("expert", "dp"), None)),
        check_vma=False,
    )
```

time: 324 us -> 200 us (0.62)
  waiting for transfers between devices: 214 us -> 6.12 us
  blocking collectives: 16.8 us -> 130 us
  starting transfers between devices: 46.7 us -> 31.2 us
  between operations: 15 us -> 2.18 us
  Pallas kernels: 12.3 us -> 21.9 us
  local copies, waits for them, and re-layouts: 12.9 us -> 4.44 us
    unnamed x3 -> x1, waiting for transfers between devices: 137 us -> 0.01 us
    ppermute x12 -> x3, waiting for transfers between devices: 71.9 us -> 0.91 us  [shift(): lax.ppermute(value, axis, [(i, (i + step) % size) for i in range(size)])]
    all_gather x0 -> x1, blocking collectives: none -> 60.5 us  [shards(): coded = lax.all_gather(coded, 'etensor', axis=0, tiled=False)]
    unnamed x0 -> x1, blocking collectives: none -> 34 us
    all_to_all x1 -> x2, blocking collectives: 16.8 us -> 35 us  [the longest x1 21.5 us: shards(): lax.all_to_all(payload, 'expert', split_axis=0, concat_axis=0, tiled=True)]
    all_to_all x1, starting transfers between devices: 13.4 us -> 3.54 us  [shards(): lax.all_to_all(back_parts(coded, down_weight, cap_rows, columns), 'dp', s...]
    pallas_call x1 -> x7, Pallas kernels: 12.3 us -> 21.9 us  [the longest x1 8.15 us: term_part(): pl.pallas_call(functools.partial(term_kernel, pitch, slots), out_shape=pl...]
    ppermute x12 -> x3, starting transfers between devices: 33.2 us -> 25.5 us  [shift(): lax.ppermute(value, axis, [(i, (i + step) % size) for i in range(size)])]
  transfers between devices with their start and end apart: 15 -> 6, of which waited for: 8 -> 2; matrix products, arithmetic and copies ran while one was open for 2% -> 2% of each run, Pallas kernels for 0% -> 5%
where the time goes in v2:
time: 200 us; the launch traced here: 197 us
  blocking collectives  130 us (65%)
  starting transfers between devices  31.2 us (16%)
  Pallas kernels  21.9 us (11%)
  waiting for transfers between devices  6.12 us (3%)
  local copies, waits for them, and re-layouts  4.44 us (2%)
  between operations  2.18 us (1%)
    all_gather x1, blocking collectives, shards(): coded = lax.all_gather(coded, 'etensor', axis=0, tiled=False)  60.5 us
    unnamed x1, blocking collectives  34 us
    ppermute x3, starting transfers between devices, shift(): lax.ppermute(value, axis, [(i, (i + step) % size) for i in range(size)])  25.5 us
    all_to_all x1, blocking collectives, shards(): lax.all_to_all(payload, 'expert', split_axis=0, concat_axis=0, tiled=True)  21.5 us
    all_to_all x1, blocking collectives, send(): lax.all_to_all(placed, 'expert', split_axis=0, concat_axis=0, tiled=True)  13.6 us
    pallas_call x1, Pallas kernels, term_part(): pl.pallas_call(functools.partial(term_kernel, pitch, slots), out_shape=pl...  8.15 us
    pallas_call x1, Pallas kernels, hidden_part(): pl.pallas_call(functools.partial(hidden_kernel, cap_rows), out_shape=(res...  5.89 us
    all_to_all x1, waiting for transfers between devices, shards(): lax.all_to_all(back_parts(coded, down_weight, cap_rows, columns), 'dp', s...  5.2 us
  transfers between devices with their start and end apart: 6, of which 2 were waited for; matrix products, arithmetic and copies ran while one was open for 2% of the time, Pallas kernels for 5%

profile of v2, /device:TPU:1, one launch (start us, length us, event | category | flops | bytes accessed | tf_op | source)
XLA Modules:
  0.0 197.1 jit_solution(10389805966894611933)
XLA Ops:
  0.6 0.0 copy-start.2
  0.6 0.8 bitcast_convert_fusion
  1.4 0.8 fusion.2
  2.3 0.0 copy-start.4
  2.3 0.0 copy-start.3
  2.3 0.8 collective-permute-start
  3.1 1.3 constant_dynamic-update-slice_fusion.1
  4.4 0.0 copy-done.2
  4.4 0.1 constant_dynamic-update-slice_fusion.refs_0_
  4.5 12.1 %collective-permute-start.1 = (bf16[2,1024,512]{2,1,0:T(8,128)(2,1)S(1)}, bf16[2,1024,512]{2,1,0:T(8,128)(2,1)}, u32[]{:S(2)}, u32[]{:S(2)}) collective-permute-start(bf16[2,1024,512]{2,1,0:T(8,128)(2,1)S(1)} %constant_dynamic-update-slice_fusion.refs_0_), channel_id=1, source_target_pairs={{0,1},{1,2},{2,3},{3,0},{4,5},{5,6},{6,7},{7,4},{8,9},{9,10},{10,1... | collective-permute-start | bytes 6291464 | tf_op jit(solution)/shard_map/ppermute | solution.py:430
  16.5 6.8 %collective-permute-start.2 = (bf16[2,1024,512]{2,1,0:T(8,128)(2,1)S(1)}, bf16[2,1024,512]{2,1,0:T(8,128)(2,1)}, u32[]{:S(2)}, u32[]{:S(2)}) collective-permute-start(bf16[2,1024,512]{2,1,0:T(8,128)(2,1)S(1)} %constant_dynamic-update-slice_fusion.refs_0_), channel_id=1, source_target_pairs={{0,3},{1,0},{2,1},{3,2},{4,7},{5,4},{6,5},{7,6},{8,11},{9,8},{10,9... | collective-permute-start | bytes 6291464 | tf_op jit(solution)/shard_map/ppermute | solution.py:430
  23.3 6.6 %collective-permute-start.3 = (bf16[2,1024,512]{2,1,0:T(8,128)(2,1)S(1)}, bf16[2,1024,512]{2,1,0:T(8,128)(2,1)}, u32[]{:S(2)}, u32[]{:S(2)}) collective-permute-start(bf16[2,1024,512]{2,1,0:T(8,128)(2,1)S(1)} %constant_dynamic-update-slice_fusion.refs_0_), channel_id=1, source_target_pairs={{0,2},{1,3},{2,0},{3,1},{4,6},{5,7},{6,4},{7,5},{8,10},{9,11},{10,... | collective-permute-start | bytes 6291464 | tf_op jit(solution)/shard_map/ppermute | solution.py:430
  30.0 0.0 copy-done.4
  30.0 0.5 slice.3
  31.1 0.0 collective-permute-done
  31.2 0.0 copy-done.3
  31.2 14.4 %conditional.1 = (s16[304,512]{1,0:T(8,128)(2,1)S(1)}, s32[2,128]{1,0:T(2,128)S(1)}) conditional(s32[]{:T(128)} %bitcast.2, () %tuple.16, (s32[128,2]{0,1:T(2,128)S(1)}, bf16[128,256]{1,0:T(8,128)(2,1)S(1)}, bf16[144,256]{1,0:T(8,128)(2,1)S(1)}) %tuple.22), branch_computations={%region_0.1_spmd, %region_1.2_spmd} | conditional | bytes 589840 | solution.py:462
  31.2 0.5 branch_1_fun.2
  31.7 13.6 %all_to_all.14.rows_hbm = bf16[8,36,512]{2,1,0:T(8,128)(2,1)S(1)} all-to-all(bf16[8,36,512]{2,1,0:T(8,128)(2,1)S(1)} %get-tuple-element.9), channel_id=1, replica_groups=mesh['expert'=8,'etensor'=16,'dp'=4] {'expert'}, dimensions={0} | all-to-all | bytes 589824 | tf_op jit(solution)/shard_map/cond/branch_1_fun/all_to_all | solution.py:459
  45.3 0.3 branch_1_fun.3
  45.6 0.0 copy-start
  45.6 60.5 %all-gather.2 = s16[4864,512]{1,0:T(8,128)(2,1)} all-gather(s16[304,512]{1,0:T(8,128)(2,1)S(1)} %get-tuple-element.20), channel_id=2, replica_groups=mesh['expert'=8,'etensor'=16,'dp'=4] {'etensor'}, dimensions={0}, use_global_device_ids=true | all-gather | bytes 5292032 | tf_op jit(solution)/shard_map/all_gather | solution.py:470
  106.2 0.0 copy-done
  106.2 4.0 %shard_map.88 = bf16[4,288,512]{2,1,0:T(8,128)(2,1)} custom-call(s16[16,304,512]{2,1,0:T(8,128)(2,1)} %bitcast.17, bf16[1,512,1024]{2,1,0:T(8,128)(2,1)S(1)} %copy-done), custom_call_target="tpu_custom_call" | custom-call | flops 1207959552 | bytes 5242880 | tf_op jit(solution)/shard_map/pallas_call | solution.py:105
  110.1 3.5 %all-to-all-start.1 = ((bf16[4,288,512]{2,1,0:T(8,128)(2,1)}), bf16[4,288,512]{2,1,0:T(8,128)(2,1)S(1)}, u32[]{:S(2)}, u32[]{:S(2)}) async-start(bf16[4,288,512]{2,1,0:T(8,128)(2,1)} %shard_map.88), calls=%async_computation.1 | async-start | bytes 2359296 | tf_op jit(solution)/shard_map/all_to_all | solution.py:472
  113.7 0.1 pad_add_fusion.slot_of
  113.8 0.0 collective-permute-done.1.refs_1_
  113.8 0.0 collective-permute-done.2.refs_2_
  113.8 0.9 collective-permute-done.3.refs_3_
  114.7 5.9 %shard_map.87 = (f32[288,512]{1,0:T(8,128)}, f32[288,512]{1,0:T(8,128)}) custom-call(s32[4]{0:T(128)S(1)} %pad_add_fusion.slot_of, s16[16,304,512]{2,1,0:T(8,128)(2,1)} %bitcast.18, bf16[2,1024,512]{2,1,0:T(8,128)(2,1)S(1)} %constant_dynamic-update-slice_fusion.refs_0_, bf16[2,1024,512]{2,1,0:T(8,128)(2,1)} %collective-permute-done.1.refs_1_, ...), custom_call_target="tpu_custom_call" | custom-call | flops 2415919104 | bytes 12582912 | tf_op jit(solution)/shard_map/pallas_call | solution.py:163
  120.6 5.2 %all-to-all-done.1.backs_hbm = bf16[4,288,512]{2,1,0:T(8,128)(2,1)S(1)} async-done(((bf16[4,288,512]{2,1,0:T(8,128)(2,1)}), bf16[4,288,512]{2,1,0:T(8,128)(2,1)S(1)}, u32[]{:S(2)}, u32[]{:S(2)}) %all-to-all-start.1) | async-done | bytes 1179680 | tf_op jit(solution)/shard_map/all_to_all | solution.py:472
  125.8 8.1 %shard_map.89 = bf16[5104,256]{1,0:T(8,128)(2,1)} custom-call(s32[4]{0:T(128)S(1)} %pad_add_fusion.slot_of, s32[1]{0:T(128)} %bitcast.9.z_of, f32[288,512]{1,0:T(8,128)} %get-tuple-element.21.gate_hbm, f32[288,512]{1,0:T(8,128)} %get-tuple-element.22.up_hbm, bf16[4,288,512]{2,1,0:T(8,128)(2,1)S(1)} %all-to-all-done.1.backs_hbm, ...), custom_call_target="tpu_custom_call" | custom-call | flops 2415919104 | bytes 14680064 | tf_op jit(solution)/shard_map/pallas_call | solution.py:262
  134.0 0.0 copy-start.1
  134.0 34.0 %fusion = bf16[320,256]{1,0:T(8,128)(2,1)S(1)} fusion(bf16[5104,256]{1,0:T(8,128)(2,1)} %shard_map.89), kind=kCustom, calls=%all-reduce-scatter | all-reduce-scatter fusion | flops 1310721 | bytes 2779136
  168.0 1.4 collective-permute-start.4
  169.4 1.3 dynamic-slice.4
  171.3 0.0 collective-permute-done.4
  171.3 0.5 concatenate.8
  171.9 0.7 constant_dynamic-slice_fusion.summed
  172.6 1.8 shard_map.90
  174.5 21.5 %all_to_all.15.came_hbm = bf16[8,48,256]{2,1,0:T(8,128)(2,1)S(1)} all-to-all(bf16[8,48,256]{2,1,0:T(8,128)(2,1)} %shard_map.90), channel_id=1, replica_groups=mesh['expert'=8,'etensor'=16,'dp'=4] {'expert'}, dimensions={0} | all-to-all | bytes 393216 | tf_op jit(solution)/shard_map/all_to_all | solution.py:488
  195.9 0.0 copy-done.1
  195.9 1.2 shard_map.91
  (1 shorter events, 0.0 us)
Async XLA Ops:
  0.6 3.7 %copy-start.2 = (bf16[1,1024,512]{2,1,0:T(8,128)(2,1)S(1)}, bf16[1,1024,512]{2,1,0:T(8,128)(2,1)}, u32[]{:S(2)}) copy-start(bf16[1,1024,512]{2,1,0:T(8,128)(2,1)} %param.14) | copy-start | bytes 3145732
  2.3 27.7 %copy-start.4 = (s32[128,2]{0,1:T(2,128)S(1)}, s32[128,2]{0,1:T(2,128)}, u32[]{:S(2)}) copy-start(s32[128,2]{0,1:T(2,128)} %param.11) | copy-start | bytes 3076
  2.3 28.9 %copy-start.3 = (bf16[128,256]{1,0:T(8,128)(2,1)S(1)}, bf16[128,256]{1,0:T(8,128)(2,1)}, u32[]{:S(2)}) copy-start(bf16[128,256]{1,0:T(8,128)(2,1)} %param.9) | copy-start | bytes 196612
  2.3 28.9 %collective-permute-start = (bf16[144,256]{1,0:T(8,128)(2,1)S(1)}, bf16[144,256]{1,0:T(8,128)(2,1)S(1)}, u32[]{:S(2)}, u32[]{:S(2)}) collective-permute-start(bf16[144,256]{1,0:T(8,128)(2,1)S(1)} %fusion.2), channel_id=1, source_target_pairs={{0,0},{1,16},{2,32},{3,48},{4,4},{5,20},{6,36},{7,52},{8,8},{9,24}... | collective-permute-start | bytes 221192 | tf_op jit(solution)/shard_map/ppermute | solution.py:455
  4.5 109.4 %collective-permute-start.1 = (bf16[2,1024,512]{2,1,0:T(8,128)(2,1)S(1)}, bf16[2,1024,512]{2,1,0:T(8,128)(2,1)}, u32[]{:S(2)}, u32[]{:S(2)}) collective-permute-start(bf16[2,1024,512]{2,1,0:T(8,128)(2,1)S(1)} %constant_dynamic-update-slice_fusion.refs_0_), channel_id=1, source_target_pairs={{0,1},{1,2},{2,3},{3,0},{4,5},{5,6},{6,7},{7,4},{8,9},{9,10},{10,1... | collective-permute-start | bytes 6291464 | tf_op jit(solution)/shard_map/ppermute | solution.py:430
  16.5 97.3 %collective-permute-start.2 = (bf16[2,1024,512]{2,1,0:T(8,128)(2,1)S(1)}, bf16[2,1024,512]{2,1,0:T(8,128)(2,1)}, u32[]{:S(2)}, u32[]{:S(2)}) collective-permute-start(bf16[2,1024,512]{2,1,0:T(8,128)(2,1)S(1)} %constant_dynamic-update-slice_fusion.refs_0_), channel_id=1, source_target_pairs={{0,3},{1,0},{2,1},{3,2},{4,7},{5,4},{6,5},{7,6},{8,11},{9,8},{10,9... | collective-permute-start | bytes 6291464 | tf_op jit(solution)/shard_map/ppermute | solution.py:430
  23.3 91.4 %collective-permute-start.3 = (bf16[2,1024,512]{2,1,0:T(8,128)(2,1)S(1)}, bf16[2,1024,512]{2,1,0:T(8,128)(2,1)}, u32[]{:S(2)}, u32[]{:S(2)}) collective-permute-start(bf16[2,1024,512]{2,1,0:T(8,128)(2,1)S(1)} %constant_dynamic-update-slice_fusion.refs_0_), channel_id=1, source_target_pairs={{0,2},{1,3},{2,0},{3,1},{4,6},{5,7},{6,4},{7,5},{8,10},{9,11},{10,... | collective-permute-start | bytes 6291464 | tf_op jit(solution)/shard_map/ppermute | solution.py:430
  45.6 60.6 %copy-start = (bf16[1,512,1024]{2,1,0:T(8,128)(2,1)S(1)}, bf16[1,512,1024]{2,1,0:T(8,128)(2,1)}, u32[]{:S(2)}) copy-start(bf16[1,512,1024]{2,1,0:T(8,128)(2,1)} %down.1) | copy-start | bytes 3145732
  110.1 15.7 %all-to-all-start.1 = ((bf16[4,288,512]{2,1,0:T(8,128)(2,1)}), bf16[4,288,512]{2,1,0:T(8,128)(2,1)S(1)}, u32[]{:S(2)}, u32[]{:S(2)}) async-start(bf16[4,288,512]{2,1,0:T(8,128)(2,1)} %shard_map.88), calls=%async_computation.1 | async-start | bytes 2359296 | tf_op jit(solution)/shard_map/all_to_all | solution.py:472
  134.0 61.9 %copy-start.1 = (f32[128,2]{0,1:T(2,128)S(1)}, f32[128,2]{0,1:T(2,128)}, u32[]{:S(2)}) copy-start(f32[128,2]{0,1:T(2,128)} %param.12) | copy-start | bytes 3076
  168.0 3.3 %collective-permute-start.4 = (bf16[15,256]{1,0:T(8,128)(2,1)S(1)}, bf16[15,256]{1,0:T(8,128)(2,1)S(1)}, u32[]{:S(2)}, u32[]{:S(2)}) collective-permute-start(bf16[15,256]{1,0:T(8,128)(2,1)S(1)} %slice.4), channel_id=1, source_target_pairs={{0,4},{4,8},{8,12},{12,16},{16,20},{20,24},{24,28},{28,32},{32,36}... | collective-permute-start | bytes 23048

commit v3 on v2

--- a/solution.py
+++ b/solution.py
@@ -29,31 +29,30 @@
     owners, capacity, both = rows.shape
     feat = both // 2
     values = jnp.concatenate([rows[e].astype(jnp.float32) for e in range(owners)], axis=0)
-    largest = jnp.max(jnp.abs(values), axis=0, keepdims=True)
-    largest = jnp.concatenate(
-        [
-            jnp.broadcast_to(jnp.max(half, axis=1, keepdims=True), (1, feat))
-            for half in (largest[:, :feat], largest[:, feat:])
-        ],
-        axis=1,
-    )
-    scale = jnp.ones((1, both), jnp.float32)
-    power = jnp.zeros((1, both), jnp.int32)
-    for step in STEPS:
-        fits = largest * (2.0**step) <= 32000.0
-        largest = jnp.where(fits, largest * (2.0**step), largest)
-        scale = jnp.where(fits, scale * (2.0**step), scale)
-        power = jnp.where(fits, power + step, power)
-    whole = jnp.round(values * scale).astype(jnp.int32)
-    tail = jnp.broadcast_to(power, (coded.shape[0] - owners * capacity, both))
-    coded[...] = jnp.concatenate([whole, tail], axis=0).astype(jnp.int16)
-
-
-def code(rows, lines):
+    count = owners * capacity
+    tails = []
+    for i, half in enumerate((values[:, feat:], values[:, :feat])):
+        largest = jnp.max(jnp.max(jnp.abs(half), axis=0, keepdims=True), axis=1, keepdims=True)
+        largest = jnp.broadcast_to(largest, (1, feat))
+        scale = jnp.ones((1, feat), jnp.float32)
+        power = jnp.zeros((1, feat), jnp.int32)
+        for step in STEPS:
+            fits = largest * (2.0**step) <= 32000.0
+            largest = jnp.where(fits, largest * (2.0**step), largest)
+            scale = jnp.where(fits, scale * (2.0**step), scale)
+            power = jnp.where(fits, power + step, power)
+        whole = jnp.round(half * scale).astype(jnp.int32)
+        coded[i * count : (i + 1) * count] = whole.astype(jnp.int16)
+        tails.append(jnp.broadcast_to(power, (8, feat)))
+    coded[2 * count :] = jnp.concatenate(tails, axis=0).astype(jnp.int16)
+
+
+def code(rows):
     owners, capacity, both = rows.shape
+    feat = both // 2
     return pl.pallas_call(
         code_kernel,
-        out_shape=jax.ShapeDtypeStruct((lines, both), jnp.int16),
+        out_shape=jax.ShapeDtypeStruct((2 * owners * capacity + 16, feat), jnp.int16),
         in_specs=[HBM],
         out_specs=VMEM,
         scratch_shapes=[pltpu.VMEM(rows.shape, rows.dtype), pltpu.SemaphoreType.DMA(())],
@@ -61,35 +60,40 @@
     )(rows)
 
 
-def decode(block, cap_rows):
-    power = block[cap_rows:].astype(jnp.int32)[0:1]
+def decode(block, tail, row):
+    power = tail.astype(jnp.int32)[row : row + 1]
     scale = jnp.ones(power.shape, jnp.float32)
     for step in STEPS:
         taken = power >= step
         scale = jnp.where(taken, scale * (0.5**step), scale)
         power = jnp.where(taken, power - step, power)
-    return (block[:cap_rows].astype(jnp.int32).astype(jnp.float32) * scale).astype(jnp.bfloat16)
-
-
-def back_kernel(cap_rows, coded, down, parts, coded_v, down_v, parts_v, sems):
+    return (block.astype(jnp.int32).astype(jnp.float32) * scale).astype(jnp.bfloat16)
+
+
+def back_kernel(coded, down, parts, coded_v, tails_v, down_v, parts_v, sems):
     groups = parts.shape[0]
     per = coded.shape[0] // groups
-    feat = coded.shape[2] // 2
+    cap_rows = parts.shape[1]
     weight = pltpu.make_async_copy(down.at[0], down_v, sems.at[groups])
+    tails = pltpu.make_async_copy(
+        coded.at[:, pl.ds(2 * cap_rows, 16)], tails_v, sems.at[2 * groups + 1]
+    )
+    tails.start()
     weight.start()
     copies = [
         pltpu.make_async_copy(
-            coded.at[pl.ds(per * g, per), :, pl.ds(feat, feat)], coded_v.at[g], sems.at[g]
+            coded.at[pl.ds(per * g, per), pl.ds(0, cap_rows)], coded_v.at[g], sems.at[g]
         )
         for g in range(groups)
     ]
     for copy in copies:
         copy.start()
+    tails.wait()
     weight.wait()
     sent = []
     for g in range(groups):
         copies[g].wait()
-        y = jnp.concatenate([decode(coded_v[g, k], cap_rows) for k in range(per)], axis=1)
+        y = jnp.concatenate([decode(coded_v[g, k], tails_v[per * g + k], 0) for k in range(per)], axis=1)
         parts_v[g] = lax.dot_general(y, down_v[...], NT, preferred_element_type=jnp.float32).astype(
             jnp.bfloat16
         )
@@ -100,18 +104,19 @@
 
 
 def back_parts(coded, down, cap_rows, groups):
-    blocks, lines, both = coded.shape
+    blocks, lines, feat = coded.shape
     _, ff, depth = down.shape
     return pl.pallas_call(
-        functools.partial(back_kernel, cap_rows),
+        back_kernel,
         out_shape=pltpu.HBM((groups, cap_rows, ff), jnp.bfloat16),
         in_specs=[HBM, HBM],
         out_specs=HBM,
         scratch_shapes=[
-            pltpu.VMEM((groups, blocks // groups, lines, both // 2), jnp.int16),
+            pltpu.VMEM((groups, blocks // groups, cap_rows, feat), jnp.int16),
+            pltpu.VMEM((blocks, 16, feat), jnp.int16),
             pltpu.VMEM((ff, depth), jnp.bfloat16),
             pltpu.VMEM((groups, cap_rows, ff), jnp.bfloat16),
-            pltpu.SemaphoreType.DMA((2 * groups + 1,)),
+            pltpu.SemaphoreType.DMA((2 * groups + 2,)),
         ],
         compiler_params=pltpu.CompilerParams(vmem_limit_bytes=24 << 20),
         cost_estimate=pl.CostEstimate(
@@ -121,72 +126,72 @@
 
 
 def hidden_kernel(cap_rows, slot_of, coded, *refs):
-    weights, (gate_out, up_out, gate_pre, up_pre, rows_v, w_v, sems) = refs[:4], refs[4:]
+    weights, (mixed, mixed_v, rows_v, tails_v, w_v, sems) = refs[:4], refs[4:]
     per = coded.shape[0] // 4
-    feat = coded.shape[2] // 2
+    ff = mixed.shape[2]
     waits = []
     for s in range(4):
-        rows = coded.at[pl.ds(slot_of[s] * per, per), :, pl.ds(0, feat)]
+        blocks = coded.at[pl.ds(slot_of[s] * per, per)]
+        rows, tails = blocks.at[:, pl.ds(cap_rows, cap_rows)], blocks.at[:, pl.ds(2 * cap_rows, 16)]
         waits.append(
             [
+                pltpu.make_async_copy(tails, tails_v.at[s], sems.at[9 + s]),
                 pltpu.make_async_copy(rows, rows_v.at[s], sems.at[2 * s]),
                 pltpu.make_async_copy(weights[s], w_v.at[s], sems.at[2 * s + 1]),
             ]
         )
         for copy in waits[s]:
             copy.start()
+    total = None
     for s in range(4):
         for copy in waits[s]:
             copy.wait()
-        x = jnp.concatenate([decode(rows_v[s, k], cap_rows) for k in range(per)], axis=1)
-        g = jnp.dot(x, w_v[s, 0], preferred_element_type=jnp.float32)
-        u = jnp.dot(x, w_v[s, 1], preferred_element_type=jnp.float32)
-        if s == 0:
-            gate_pre[...], up_pre[...] = g, u
-        else:
-            gate_pre[...] += g
-            up_pre[...] += u
-    sent = [
-        pltpu.make_async_copy(gate_pre, gate_out, sems.at[8]),
-        pltpu.make_async_copy(up_pre, up_out, sems.at[9]),
-    ]
-    for copy in sent:
-        copy.start()
-    for copy in sent:
-        copy.wait()
+        x = jnp.concatenate([decode(rows_v[s, k], tails_v[s, k], 8) for k in range(per)], axis=1)
+        part = jnp.dot(x, w_v[s], preferred_element_type=jnp.float32)
+        total = part if s == 0 else total + part
+    gate_pre, up_pre = total[:, :ff], total[:, ff:]
+    sig = 1.0 / (1.0 + jnp.exp(-gate_pre))
+    act = gate_pre * sig
+    mixed_v[0] = up_pre * sig * (1.0 + gate_pre * (1.0 - sig))
+    mixed_v[1] = act
+    mixed_v[2] = act * up_pre
+    sent = pltpu.make_async_copy(mixed_v, mixed, sems.at[8])
+    sent.start()
+    sent.wait()
 
 
 def hidden_part(coded, weights, slot_of, cap_rows):
-    blocks, lines, both = coded.shape
-    _, depth, ff = weights[0].shape
-    result = pltpu.HBM((cap_rows, ff), jnp.float32)
+    blocks, lines, feat = coded.shape
+    depth, wide = weights[0].shape
     return pl.pallas_call(
         functools.partial(hidden_kernel, cap_rows),
-        out_shape=(result, result),
+        out_shape=pltpu.HBM((3, cap_rows, wide // 2), jnp.float32),
         in_specs=[SMEM] + [HBM] * 5,
-        out_specs=(HBM, HBM),
+        out_specs=HBM,
         scratch_shapes=[
-            pltpu.VMEM((cap_rows, ff), jnp.float32),
-            pltpu.VMEM((cap_rows, ff), jnp.float32),
-            pltpu.VMEM((4, blocks // 4, lines, both // 2), jnp.int16),
-            pltpu.VMEM((4, 2, depth, ff), jnp.bfloat16),
-            pltpu.SemaphoreType.DMA((10,)),
+            pltpu.VMEM((3, cap_rows, wide // 2), jnp.float32),
+            pltpu.VMEM((4, blocks // 4, cap_rows, feat), jnp.int16),
+            pltpu.VMEM((4, blocks // 4, 16, feat), jnp.int16),
+            pltpu.VMEM((4, depth, wide), jnp.bfloat16),
+            pltpu.SemaphoreType.DMA((13,)),
         ],
         compiler_params=pltpu.CompilerParams(vmem_limit_bytes=32 << 20),
         cost_estimate=pl.CostEstimate(
-            flops=4 * cap_rows * 4 * depth * ff, bytes_accessed=12 << 20, transcendentals=0
+            flops=8 * cap_rows * depth * wide,
+            bytes_accessed=12 << 20,
+            transcendentals=cap_rows * wide // 2,
         ),
     )(slot_of, coded, *weights)
 
 
-def term_kernel(pitch, slots, slot_of, z_of, gate_hbm, up_hbm, backs_hbm, *refs):
-    weights, (out, gate_ref, up_ref, backs, w_v, out_v, blank, sems) = refs[:4], refs[4:]
-    cap_rows = gate_ref.shape[0]
+def term_kernel(pitch, slots, slot_of, z_of, mixed_hbm, backs_hbm, *refs):
+    weights, (out, mixed, backs, w_v, out_v, blank, sems) = refs[:4], refs[4:]
+    cap_rows = mixed.shape[1]
     feat = out.shape[1]
-    per = w_v.shape[2] // feat
+    per = w_v.shape[1] // feat
     first = [
-        pltpu.make_async_copy(src, dst, sems.at[4 + i])
-        for i, (src, dst) in enumerate(((gate_hbm, gate_ref), (up_hbm, up_ref), (backs_hbm, backs)))
+        pltpu.make_async_copy(backs_hbm, backs, sems.at[4]),
+        pltpu.make_async_copy(mixed_hbm, mixed, sems.at[5]),
     ]
     for copy in first:
         copy.start()
@@ -195,15 +200,13 @@
         copy.start()
     for copy in first:
         copy.wait()
-    gate_pre, up_pre = gate_ref[...], up_ref[...]
     for s in range(4):
         b = backs[s].astype(jnp.float32)
         back = b if s == 0 else back + b
-    sig = 1.0 / (1.0 + jnp.exp(-gate_pre))
-    act = gate_pre * sig
-    prod = act * up_pre * back
-    d_gate = (back * up_pre * sig * (1.0 + gate_pre * (1.0 - sig))).astype(jnp.bfloat16)
-    d_up = (back * act).astype(jnp.bfloat16)
+    prod = mixed[2] * back
+    sides = jnp.concatenate(
+        [(back * mixed[0]).astype(jnp.bfloat16), (back * mixed[1]).astype(jnp.bfloat16)], axis=1
+    )
 
     ones = jnp.ones((16, prod.shape[1]), jnp.bfloat16)
     total = None
@@ -239,8 +242,7 @@
         sent[j].start()
     for s in range(4):
         waits[s].wait()
-        term = lax.dot_general(d_gate, w_v[s, 0], NT, preferred_element_type=jnp.float32)
-        term = term + lax.dot_general(d_up, w_v[s, 1], NT, preferred_element_type=jnp.float32)
+        term = lax.dot_general(sides, w_v[s], NT, preferred_element_type=jnp.float32)
         for k in range(per):
             at = k * pitch
             out_v[s, at : at + cap_rows] = term[:, k * feat : (k + 1) * feat].astype(jnp.bfloat16)
@@ -254,30 +256,50 @@
         copy.wait()
 
 
-def term_part(gate_pre, up_pre, backs, weights, slot_of, z_index, feat, pitch, out_rows, slots):
-    cap_rows, ff = gate_pre.shape
-    depth = weights[0].shape[1]
+def term_part(mixed, backs, weights, slot_of, z_index, feat, pitch, out_rows, slots):
+    _, cap_rows, ff = mixed.shape
+    depth, wide = weights[0].shape
     z_of = jnp.reshape(z_index % slots, (1,)).astype(jnp.int32)
     per = depth // feat
     return pl.pallas_call(
         functools.partial(term_kernel, pitch, slots),
         out_shape=pltpu.HBM((out_rows, feat), jnp.bfloat16),
-        in_specs=[SMEM, SMEM] + [HBM] * 7,
+        in_specs=[SMEM, SMEM] + [HBM] * 6,
         out_specs=HBM,
         scratch_shapes=[
-            pltpu.VMEM((cap_rows, ff), jnp.float32),
-            pltpu.VMEM((cap_rows, ff), jnp.float32),
+            pltpu.VMEM((3, cap_rows, ff), jnp.float32),
             pltpu.VMEM((4, cap_rows, ff), jnp.bfloat16),
-            pltpu.VMEM((4, 2, depth, ff), jnp.bfloat16),
+            pltpu.VMEM((4, depth, wide), jnp.bfloat16),
             pltpu.VMEM((4, per * pitch - 16, feat), jnp.bfloat16),
             pltpu.VMEM((16, feat), jnp.bfloat16),
             pltpu.SemaphoreType.DMA((14,)),
         ],
         compiler_params=pltpu.CompilerParams(vmem_limit_bytes=40 << 20),
         cost_estimate=pl.CostEstimate(
-            flops=4 * cap_rows * 4 * depth * ff, bytes_accessed=14 << 20, transcendentals=cap_rows * ff
-        ),
-    )(slot_of, z_of, gate_pre, up_pre, backs, *weights)
+            flops=8 * cap_rows * depth * wide, bytes_accessed=14 << 20, transcendentals=0
+        ),
+    )(slot_of, z_of, mixed, backs, *weights)
+
+
+def tag_kernel(out_grad, routes, tagged):
+    tok_rows, feat = out_grad.shape
+    tagged[:tok_rows] = out_grad[...]
+    lines = routes[...].astype(jnp.float32)
+    lines = jnp.concatenate([lines, jnp.zeros((2, feat - tok_rows), jnp.float32)], axis=1)
+    row = lax.broadcasted_iota(jnp.int32, (16, feat), 0)
+    tags = jnp.where(row == 0, lines[0:1], jnp.where(row == 1, lines[1:2], 0.0))
+    tagged[tok_rows:] = tags.astype(jnp.bfloat16)
+
+
+def tag(out_grad, routes):
+    tok_rows, feat = out_grad.shape
+    return pl.pallas_call(
+        tag_kernel,
+        out_shape=jax.ShapeDtypeStruct((tok_rows + 16, feat), jnp.bfloat16),
+        in_specs=[VMEM, VMEM],
+        out_specs=VMEM,
+        compiler_params=pltpu.CompilerParams(vmem_limit_bytes=8 << 20),
+    )(out_grad, routes)
 
 
 def place_kernel(capacity, routes, tokens, moved_hbm, placed, slot, moved, sem):
@@ -442,7 +464,7 @@
     slots = 7
 
     columns = lax.axis_size("dp")
-    gate_up = jnp.concatenate([gate_weight, up_weight], axis=0)
+    gate_up = jnp.concatenate([gate_weight[0], up_weight[0]], axis=1)
 
     per = blocks // columns
     swap = [
@@ -451,19 +473,18 @@
         for w in range(per)
         for x in range(columns)
     ]
-    tags = jnp.pad(routes.T.astype(jnp.bfloat16), ((0, 14), (0, feat - tok_rows)))
-    moved = lax.ppermute(jnp.concatenate([out_grad, tags], axis=0), ("etensor", "dp"), swap)
+    moved = lax.ppermute(tag(out_grad, routes.T), ("etensor", "dp"), swap)
 
     def send():
         placed, slot = place(routes.T, tokens, moved, experts, capacity)
         part = lax.all_to_all(placed, "expert", split_axis=0, concat_axis=0, tiled=True)
-        return code(part, cap_rows + 16), slot
+        return code(part), slot
 
     coded, slot = lax.cond(
-        routes[0, 0] >= 0,
+        x_index >= 0,
         send,
         lambda: (
-            jnp.zeros((cap_rows + 16, 2 * feat), jnp.int16),
+            jnp.zeros((2 * cap_rows + 16, feat), jnp.int16),
             jnp.zeros((2, tok_rows), jnp.int32),
         ),
     )
@@ -473,15 +494,14 @@
         back_parts(coded, down_weight, cap_rows, columns), "dp", split_axis=0, concat_axis=0, tiled=True
     )
 
-    weights = (gate_up,) + tuple(shift(gate_up, "dp", step) for step in (1, -1, 2))
-    slot_of = jnp.stack([(x_index + step) % 4 for step in (0, 3, 1, 2)]).astype(jnp.int32)
-    gate_pre, up_pre = (
-        pltpu.with_memory_space_constraint(v, pltpu.HBM)
-        for v in hidden_part(coded, weights, slot_of, cap_rows)
+    weights = (gate_up,) + tuple(shift(gate_up, "dp", step) for step in (2, 1, -1))
+    slot_of = jnp.stack([(x_index + step) % 4 for step in (0, 2, 3, 1)]).astype(jnp.int32)
+    mixed = pltpu.with_memory_space_constraint(
+        hidden_part(coded, weights, slot_of, cap_rows), pltpu.HBM
     )
     pitch = cap_rows + 32
     terms = term_part(
-        gate_pre, up_pre, backs, weights, slot_of, z_index, feat, pitch, blocks * (pitch - 1), slots
+        mixed, backs, weights, slot_of, z_index, feat, pitch, blocks * (pitch - 1), slots
     )
     summed = lax.psum_scatter(terms, "etensor", scatter_dimension=0, tiled=True)
     payload = pack(summed, z_index, owners, capacity, slots, 48)

time: 200 us -> 198 us (0.990)
  blocking collectives: 130 us -> 127 us
  starting transfers between devices: 31.2 us -> 33.3 us
    all_to_all x1, blocking collectives: 21.5 us -> 19.3 us  [shards(): lax.all_to_all(payload, 'expert', split_axis=0, concat_axis=0, tiled=True)]
    pallas_call x3 -> x4, Pallas kernels: 10.2 us -> 11.9 us  [the longest x1 6.86 us: hidden_part(): pl.pallas_call(functools.partial(hidden_kernel, cap_rows), out_shape=pltp...]
  transfers between devices with their start and end apart: 6 -> 6, of which waited for: 2 -> 2; matrix products, arithmetic and copies ran while one was open for 2% -> 2% of each run, Pallas kernels for 5% -> 6%
where the time goes in v3:
time: 198 us; the launch traced here: 196 us
  blocking collectives  127 us (64%)
  starting transfers between devices  33.3 us (17%)
  Pallas kernels  22.8 us (12%)
  waiting for transfers between devices  5.91 us (3%)
  local copies, waits for them, and re-layouts  3.38 us (2%)
    all_gather x1, blocking collectives, shards(): coded = lax.all_gather(coded, 'etensor', axis=0, tiled=False)  60.7 us
    unnamed x1, blocking collectives  33.4 us
    ppermute x3, starting transfers between devices, shift(): lax.ppermute(value, axis, [(i, (i + step) % size) for i in range(size)])  26.7 us
    all_to_all x1, blocking collectives, shards(): lax.all_to_all(payload, 'expert', split_axis=0, concat_axis=0, tiled=True)  19.3 us
    all_to_all x1, blocking collectives, send(): lax.all_to_all(placed, 'expert', split_axis=0, concat_axis=0, tiled=True)  13.9 us
    pallas_call x1, Pallas kernels, term_part(): pl.pallas_call(functools.partial(term_kernel, pitch, slots), out_shape=pl...  7.4 us
    pallas_call x1, Pallas kernels, hidden_part(): pl.pallas_call(functools.partial(hidden_kernel, cap_rows), out_shape=pltp...  6.86 us
    all_to_all x1, waiting for transfers between devices, shards(): lax.all_to_all(back_parts(coded, down_weight, cap_rows, columns), 'dp', s...  4.5 us
  transfers between devices with their start and end apart: 6, of which 2 were waited for; matrix products, arithmetic and copies ran while one was open for 2% of the time, Pallas kernels for 6%

profile of v3, /device:TPU:1, one launch (start us, length us, event | category | flops | bytes accessed | tf_op | source)
XLA Modules:
  0.0 196.2 jit_solution(6545793737277798891)
XLA Ops:
  0.6 0.0 copy-start.1
  0.6 0.8 copy-done.1
  1.5 0.7 shard_map.87
  2.2 0.7 collective-permute-start
  2.8 0.0 copy-start.3
  2.8 0.0 copy-start.4
  2.8 1.8 pad_maximum_fusion.refs_0_
  4.7 20.2 %collective-permute-start.1 = (bf16[1024,1024]{1,0:T(8,128)(2,1)S(1)}, bf16[1024,1024]{1,0:T(8,128)(2,1)}, u32[]{:S(2)}, u32[]{:S(2)}) collective-permute-start(bf16[1024,1024]{1,0:T(8,128)(2,1)S(1)} %pad_maximum_fusion.refs_0_), channel_id=1, source_target_pairs={{0,2},{1,3},{2,0},{3,1},{4,6},{5,7},{6,4},{7,5},{8,10},{9,11},{10,... | collective-permute-start | bytes 6291464 | tf_op jit(solution)/shard_map/ppermute | solution.py:452
  24.9 1.9 collective-permute-start.2
  26.8 4.6 %collective-permute-start.3 = (bf16[1024,1024]{1,0:T(8,128)(2,1)S(1)}, bf16[1024,1024]{1,0:T(8,128)(2,1)}, u32[]{:S(2)}, u32[]{:S(2)}) collective-permute-start(bf16[1024,1024]{1,0:T(8,128)(2,1)S(1)} %pad_maximum_fusion.refs_0_), channel_id=1, source_target_pairs={{0,3},{1,0},{2,1},{3,2},{4,7},{5,4},{6,5},{7,6},{8,11},{9,8},{10,9... | collective-permute-start | bytes 6291464 | tf_op jit(solution)/shard_map/ppermute | solution.py:452
  31.4 0.0 collective-permute-done
  31.4 0.0 copy-done.3
  31.4 0.0 copy-done.4
  31.4 14.8 %conditional.1 = (s16[592,256]{1,0:T(8,128)(2,1)S(1)}, s32[2,128]{1,0:T(2,128)S(1)}) conditional(s32[]{:T(128)} %convert_element_type.3, () %tuple.16, (s32[128,2]{0,1:T(2,128)S(1)}, bf16[128,256]{1,0:T(8,128)(2,1)S(1)}, bf16[144,256]{1,0:T(8,128)(2,1)S(1)}) %tuple.22), branch_computations={%region_0.0_spmd, %region_1.0_spmd} | conditional | bytes 589840 | solution.py:483
  31.4 0.5 branch_1_fun.2
  32.0 13.9 %all_to_all.14.rows_hbm = bf16[8,36,512]{2,1,0:T(8,128)(2,1)S(1)} all-to-all(bf16[8,36,512]{2,1,0:T(8,128)(2,1)S(1)} %get-tuple-element.9), channel_id=1, replica_groups=mesh['expert'=8,'etensor'=16,'dp'=4] {'expert'}, dimensions={0} | all-to-all | bytes 589824 | tf_op jit(solution)/shard_map/cond/branch_1_fun/all_to_all | solution.py:480
  45.9 0.3 branch_1_fun.3
  46.2 0.0 copy-start
  46.2 60.7 %all-gather.2 = s16[9472,256]{1,0:T(8,128)(2,1)} all-gather(s16[592,256]{1,0:T(8,128)(2,1)S(1)} %get-tuple-element.18), channel_id=2, replica_groups=mesh['expert'=8,'etensor'=16,'dp'=4] {'etensor'}, dimensions={0}, use_global_device_ids=true | all-gather | bytes 5152768 | tf_op jit(solution)/shard_map/all_gather | solution.py:491
  106.9 0.0 copy-done
  106.9 4.0 %shard_map.89 = bf16[4,288,512]{2,1,0:T(8,128)(2,1)} custom-call(s16[16,592,256]{2,1,0:T(8,128)(2,1)} %bitcast.17, bf16[1,512,1024]{2,1,0:T(8,128)(2,1)S(1)} %copy-done), custom_call_target="tpu_custom_call" | custom-call | flops 1207959552 | bytes 5242880 | tf_op jit(solution)/shard_map/pallas_call | solution.py:109
  110.9 3.5 %all-to-all-start.1 = ((bf16[4,288,512]{2,1,0:T(8,128)(2,1)}), bf16[4,288,512]{2,1,0:T(8,128)(2,1)S(1)}, u32[]{:S(2)}, u32[]{:S(2)}) async-start(bf16[4,288,512]{2,1,0:T(8,128)(2,1)} %shard_map.89), calls=%async_computation.1 | async-start | bytes 2359296 | tf_op jit(solution)/shard_map/all_to_all | solution.py:493
  114.5 0.1 pad_add_fusion.slot_of
  114.6 0.0 collective-permute-done.1.refs_1_
  114.6 1.4 collective-permute-done.2.refs_2_
  116.0 0.0 collective-permute-done.3.refs_3_
  116.0 6.9 %shard_map.88.mixed_hbm = f32[3,288,512]{2,1,0:T(8,128)} custom-call(s32[4]{0:T(128)S(1)} %pad_add_fusion.slot_of, s16[16,592,256]{2,1,0:T(8,128)(2,1)} %bitcast.18, bf16[1024,1024]{1,0:T(8,128)(2,1)S(1)} %pad_maximum_fusion.refs_0_, bf16[1024,1024]{1,0:T(8,128)(2,1)} %collective-permute-done.1.refs_1_, bf16[1024,1024]{1,0:T(8,128)(2,1)} %collective-permute-done.2.refs_2_, ...), custom_call_target="tpu_custom_call" | custom-call | flops 2415919104 | bytes 12582912 | tf_op jit(solution)/shard_map/pallas_call | solution.py:166
  122.9 4.5 %all-to-all-done.1.backs_hbm = bf16[4,288,512]{2,1,0:T(8,128)(2,1)S(1)} async-done(((bf16[4,288,512]{2,1,0:T(8,128)(2,1)}), bf16[4,288,512]{2,1,0:T(8,128)(2,1)S(1)}, u32[]{:S(2)}, u32[]{:S(2)}) %all-to-all-start.1) | async-done | bytes 1179680 | tf_op jit(solution)/shard_map/all_to_all | solution.py:493
  127.4 7.4 %shard_map.90 = bf16[5104,256]{1,0:T(8,128)(2,1)} custom-call(s32[4]{0:T(128)S(1)} %pad_add_fusion.slot_of, s32[1]{0:T(128)} %bitcast.8.z_of, f32[3,288,512]{2,1,0:T(8,128)} %shard_map.88.mixed_hbm, bf16[4,288,512]{2,1,0:T(8,128)(2,1)S(1)} %all-to-all-done.1.backs_hbm, bf16[1024,1024]{1,0:T(8,128)(2,1)S(1)} %pad_maximum_fusion.refs_0_, ...), custom_call_target="tpu_custom_call" | custom-call | flops 2415919104 | bytes 14680064 | tf_op jit(solution)/shard_map/pallas_call | solution.py:264
  134.8 0.0 copy-start.2
  134.8 33.4 %fusion = bf16[320,256]{1,0:T(8,128)(2,1)S(1)} fusion(bf16[5104,256]{1,0:T(8,128)(2,1)} %shard_map.90), kind=kCustom, calls=%all-reduce-scatter | all-reduce-scatter fusion | flops 1310721 | bytes 2779136
  168.3 2.4 %collective-permute-start.4 = (bf16[15,256]{1,0:T(8,128)(2,1)S(1)}, bf16[15,256]{1,0:T(8,128)(2,1)S(1)}, u32[]{:S(2)}, u32[]{:S(2)}) collective-permute-start(bf16[15,256]{1,0:T(8,128)(2,1)S(1)} %slice), channel_id=1, source_target_pairs={{0,4},{4,8},{8,12},{12,16},{16,20},{20,24},{24,28},{28,32},{32,36}... | collective-permute-start | bytes 23048
  170.7 1.3 dynamic-slice.4
  172.6 0.0 collective-permute-done.4
  172.6 0.5 concatenate.4
  173.2 0.7 constant_dynamic-slice_fusion.summed
  173.9 1.8 shard_map.91
  175.7 19.3 %all_to_all.15.came_hbm = bf16[8,48,256]{2,1,0:T(8,128)(2,1)S(1)} all-to-all(bf16[8,48,256]{2,1,0:T(8,128)(2,1)} %shard_map.91), channel_id=1, replica_groups=mesh['expert'=8,'etensor'=16,'dp'=4] {'expert'}, dimensions={0} | all-to-all | bytes 393216 | tf_op jit(solution)/shard_map/all_to_all | solution.py:508
  195.0 0.0 copy-done.2
  195.0 1.2 shard_map.92
  (1 shorter events, 0.0 us)
Async XLA Ops:
  0.6 0.8 copy-start.1
  2.2 29.3 %collective-permute-start = (bf16[144,256]{1,0:T(8,128)(2,1)S(1)}, bf16[144,256]{1,0:T(8,128)(2,1)S(1)}, u32[]{:S(2)}, u32[]{:S(2)}) collective-permute-start(bf16[144,256]{1,0:T(8,128)(2,1)S(1)} %shard_map.87), channel_id=1, source_target_pairs={{0,0},{1,16},{2,32},{3,48},{4,4},{5,20},{6,36},{7,52},{8,8},{9,24}... | collective-permute-start | bytes 221192 | tf_op jit(solution)/shard_map/ppermute | solution.py:476
  2.8 28.6 %copy-start.3 = (bf16[128,256]{1,0:T(8,128)(2,1)S(1)}, bf16[128,256]{1,0:T(8,128)(2,1)}, u32[]{:S(2)}) copy-start(bf16[128,256]{1,0:T(8,128)(2,1)} %param.9) | copy-start | bytes 196612
  2.8 28.6 %copy-start.4 = (s32[128,2]{0,1:T(2,128)S(1)}, s32[128,2]{0,1:T(2,128)}, u32[]{:S(2)}) copy-start(s32[128,2]{0,1:T(2,128)} %param.11) | copy-start | bytes 3076
  4.7 109.9 %collective-permute-start.1 = (bf16[1024,1024]{1,0:T(8,128)(2,1)S(1)}, bf16[1024,1024]{1,0:T(8,128)(2,1)}, u32[]{:S(2)}, u32[]{:S(2)}) collective-permute-start(bf16[1024,1024]{1,0:T(8,128)(2,1)S(1)} %pad_maximum_fusion.refs_0_), channel_id=1, source_target_pairs={{0,2},{1,3},{2,0},{3,1},{4,6},{5,7},{6,4},{7,5},{8,10},{9,11},{10,... | collective-permute-start | bytes 6291464 | tf_op jit(solution)/shard_map/ppermute | solution.py:452
  24.9 91.1 %collective-permute-start.2 = (bf16[1024,1024]{1,0:T(8,128)(2,1)S(1)}, bf16[1024,1024]{1,0:T(8,128)(2,1)}, u32[]{:S(2)}, u32[]{:S(2)}) collective-permute-start(bf16[1024,1024]{1,0:T(8,128)(2,1)S(1)} %pad_maximum_fusion.refs_0_), channel_id=1, source_target_pairs={{0,1},{1,2},{2,3},{3,0},{4,5},{5,6},{6,7},{7,4},{8,9},{9,10},{10,1... | collective-permute-start | bytes 6291464 | tf_op jit(solution)/shard_map/ppermute | solution.py:452
  26.8 89.2 %collective-permute-start.3 = (bf16[1024,1024]{1,0:T(8,128)(2,1)S(1)}, bf16[1024,1024]{1,0:T(8,128)(2,1)}, u32[]{:S(2)}, u32[]{:S(2)}) collective-permute-start(bf16[1024,1024]{1,0:T(8,128)(2,1)S(1)} %pad_maximum_fusion.refs_0_), channel_id=1, source_target_pairs={{0,3},{1,0},{2,1},{3,2},{4,7},{5,4},{6,5},{7,6},{8,11},{9,8},{10,9... | collective-permute-start | bytes 6291464 | tf_op jit(solution)/shard_map/ppermute | solution.py:452
  46.2 60.7 %copy-start = (bf16[1,512,1024]{2,1,0:T(8,128)(2,1)S(1)}, bf16[1,512,1024]{2,1,0:T(8,128)(2,1)}, u32[]{:S(2)}) copy-start(bf16[1,512,1024]{2,1,0:T(8,128)(2,1)} %down.1) | copy-start | bytes 3145732
  110.9 16.5 %all-to-all-start.1 = ((bf16[4,288,512]{2,1,0:T(8,128)(2,1)}), bf16[4,288,512]{2,1,0:T(8,128)(2,1)S(1)}, u32[]{:S(2)}, u32[]{:S(2)}) async-start(bf16[4,288,512]{2,1,0:T(8,128)(2,1)} %shard_map.89), calls=%async_computation.1 | async-start | bytes 2359296 | tf_op jit(solution)/shard_map/all_to_all | solution.py:493
  134.8 60.2 %copy-start.2 = (f32[128,2]{0,1:T(2,128)S(1)}, f32[128,2]{0,1:T(2,128)}, u32[]{:S(2)}) copy-start(f32[128,2]{0,1:T(2,128)} %param.12) | copy-start | bytes 3076
  168.3 4.4 %collective-permute-start.4 = (bf16[15,256]{1,0:T(8,128)(2,1)S(1)}, bf16[15,256]{1,0:T(8,128)(2,1)S(1)}, u32[]{:S(2)}, u32[]{:S(2)}) collective-permute-start(bf16[15,256]{1,0:T(8,128)(2,1)S(1)} %slice), channel_id=1, source_target_pairs={{0,4},{4,8},{8,12},{12,16},{16,20},{20,24},{24,28},{28,32},{32,36}... | collective-permute-start | bytes 23048

commit v4 on v3

--- a/solution.py
+++ b/solution.py
@@ -447,9 +447,8 @@
     )(routes, slot, probs, came)
 
 
-def shift(value, axis, step):
-    size = lax.axis_size(axis)
-    return lax.ppermute(value, axis, [(i, (i + step) % size) for i in range(size)])
+def trade(value, axis, bits):
+    return lax.ppermute(value, axis, [(i, i ^ bits) for i in range(lax.axis_size(axis))])
 
 
 def shards(tokens, out_grad, routes, gate_probs, gate_weight, up_weight, down_weight):
@@ -494,8 +493,8 @@
         back_parts(coded, down_weight, cap_rows, columns), "dp", split_axis=0, concat_axis=0, tiled=True
     )
 
-    weights = (gate_up,) + tuple(shift(gate_up, "dp", step) for step in (2, 1, -1))
-    slot_of = jnp.stack([(x_index + step) % 4 for step in (0, 2, 3, 1)]).astype(jnp.int32)
+    weights = (gate_up,) + tuple(trade(gate_up, "dp", bits) for bits in (2, 1, 3))
+    slot_of = jnp.stack([x_index ^ bits for bits in (0, 2, 1, 3)]).astype(jnp.int32)
     mixed = pltpu.with_memory_space_constraint(
         hidden_part(coded, weights, slot_of, cap_rows), pltpu.HBM
     )

time: 198 us -> 198 us (level)
  blocking collectives: 127 us -> 129 us
    all_to_all x1, waiting for transfers between devices: 4.5 us -> 2 us  [shards(): lax.all_to_all(back_parts(coded, down_weight, cap_rows, columns), 'dp', s...]
    ppermute x3, starting transfers between devices: 26.7 us -> 24.3 us  [trade(): lax.ppermute(value, axis, [(i, i ^ bits) for i in range(lax.axis_size(axi...]
    ppermute x3, waiting for transfers between devices: 1.4 us -> 3.74 us  [trade(): lax.ppermute(value, axis, [(i, i ^ bits) for i in range(lax.axis_size(axi...]
    all_to_all x1, blocking collectives: 19.3 us -> 21.3 us  [shards(): lax.all_to_all(payload, 'expert', split_axis=0, concat_axis=0, tiled=True)]
  transfers between devices with their start and end apart: 6 -> 6, of which waited for: 2 -> 3; matrix products, arithmetic and copies ran while one was open for 2% -> 2% of each run, Pallas kernels for 6% -> 6%
where the time goes in v4:
time: 198 us; the launch traced here: 196 us
  blocking collectives  129 us (65%)
  starting transfers between devices  31.6 us (16%)
  Pallas kernels  22.8 us (12%)
  waiting for transfers between devices  5.74 us (3%)
  local copies, waits for them, and re-layouts  3.38 us (2%)
    all_gather x1, blocking collectives, shards(): coded = lax.all_gather(coded, 'etensor', axis=0, tiled=False)  60.4 us
    unnamed x1, blocking collectives  33.9 us
    ppermute x3, starting transfers between devices, trade(): lax.ppermute(value, axis, [(i, i ^ bits) for i in range(lax.axis_size(axi...  24.3 us
    all_to_all x1, blocking collectives, shards(): lax.all_to_all(payload, 'expert', split_axis=0, concat_axis=0, tiled=True)  21.3 us
    all_to_all x1, blocking collectives, send(): lax.all_to_all(placed, 'expert', split_axis=0, concat_axis=0, tiled=True)  13.6 us
    pallas_call x1, Pallas kernels, term_part(): pl.pallas_call(functools.partial(term_kernel, pitch, slots), out_shape=pl...  7.39 us
    pallas_call x1, Pallas kernels, hidden_part(): pl.pallas_call(functools.partial(hidden_kernel, cap_rows), out_shape=pltp...  6.86 us
    all_to_all x1, starting transfers between devices, shards(): lax.all_to_all(back_parts(coded, down_weight, cap_rows, columns), 'dp', s...  4.21 us
  transfers between devices with their start and end apart: 6, of which 3 were waited for; matrix products, arithmetic and copies ran while one was open for 2% of the time, Pallas kernels for 6%

profile of v4, /device:TPU:1, one launch (start us, length us, event | category | flops | bytes accessed | tf_op | source)
XLA Modules:
  0.0 196.2 jit_solution(14251619269052746037)
XLA Ops:
  0.6 0.0 copy-start.1
  0.6 0.8 copy-done.1
  1.5 0.7 shard_map.87
  2.2 0.7 collective-permute-start
  2.8 0.0 copy-start.3
  2.8 0.0 copy-start.4
  2.8 1.8 pad_maximum_fusion.refs_0_
  4.7 20.2 %collective-permute-start.1 = (bf16[1024,1024]{1,0:T(8,128)(2,1)S(1)}, bf16[1024,1024]{1,0:T(8,128)(2,1)}, u32[]{:S(2)}, u32[]{:S(2)}) collective-permute-start(bf16[1024,1024]{1,0:T(8,128)(2,1)S(1)} %pad_maximum_fusion.refs_0_), channel_id=1, source_target_pairs={{0,2},{1,3},{2,0},{3,1},{4,6},{5,7},{6,4},{7,5},{8,10},{9,11},{10,... | collective-permute-start | bytes 6291464 | tf_op jit(solution)/shard_map/ppermute | solution.py:451
  24.9 1.9 collective-permute-start.2
  26.8 2.2 %collective-permute-start.3 = (bf16[1024,1024]{1,0:T(8,128)(2,1)S(1)}, bf16[1024,1024]{1,0:T(8,128)(2,1)}, u32[]{:S(2)}, u32[]{:S(2)}) collective-permute-start(bf16[1024,1024]{1,0:T(8,128)(2,1)S(1)} %pad_maximum_fusion.refs_0_), channel_id=1, source_target_pairs={{0,3},{1,2},{2,1},{3,0},{4,7},{5,6},{6,5},{7,4},{8,11},{9,10},{10,... | collective-permute-start | bytes 6291464 | tf_op jit(solution)/shard_map/ppermute | solution.py:451
  29.0 0.0 collective-permute-done
  29.0 0.0 copy-done.3
  29.1 0.0 copy-done.4
  29.1 14.5 %conditional.1 = (s16[592,256]{1,0:T(8,128)(2,1)S(1)}, s32[2,128]{1,0:T(2,128)S(1)}) conditional(s32[]{:T(128)} %convert_element_type.3, () %tuple.16, (s32[128,2]{0,1:T(2,128)S(1)}, bf16[128,256]{1,0:T(8,128)(2,1)S(1)}, bf16[144,256]{1,0:T(8,128)(2,1)S(1)}) %tuple.22), branch_computations={%region_0.0_spmd, %region_1.0_spmd} | conditional | bytes 589840 | solution.py:482
  29.1 0.5 branch_1_fun.2
  29.6 13.6 %all_to_all.14.rows_hbm = bf16[8,36,512]{2,1,0:T(8,128)(2,1)S(1)} all-to-all(bf16[8,36,512]{2,1,0:T(8,128)(2,1)S(1)} %get-tuple-element.9), channel_id=1, replica_groups=mesh['expert'=8,'etensor'=16,'dp'=4] {'expert'}, dimensions={0} | all-to-all | bytes 589824 | tf_op jit(solution)/shard_map/cond/branch_1_fun/all_to_all | solution.py:479
  43.2 0.3 branch_1_fun.3
  43.6 0.0 copy-start
  43.6 60.4 %all-gather.2 = s16[9472,256]{1,0:T(8,128)(2,1)} all-gather(s16[592,256]{1,0:T(8,128)(2,1)S(1)} %get-tuple-element.18), channel_id=2, replica_groups=mesh['expert'=8,'etensor'=16,'dp'=4] {'etensor'}, dimensions={0}, use_global_device_ids=true | all-gather | bytes 5152768 | tf_op jit(solution)/shard_map/all_gather | solution.py:490
  104.0 0.0 copy-done
  104.0 4.0 %shard_map.89 = bf16[4,288,512]{2,1,0:T(8,128)(2,1)} custom-call(s16[16,592,256]{2,1,0:T(8,128)(2,1)} %bitcast.17, bf16[1,512,1024]{2,1,0:T(8,128)(2,1)S(1)} %copy-done), custom_call_target="tpu_custom_call" | custom-call | flops 1207959552 | bytes 5242880 | tf_op jit(solution)/shard_map/pallas_call | solution.py:109
  108.0 4.2 %all-to-all-start.1 = ((bf16[4,288,512]{2,1,0:T(8,128)(2,1)}), bf16[4,288,512]{2,1,0:T(8,128)(2,1)S(1)}, u32[]{:S(2)}, u32[]{:S(2)}) async-start(bf16[4,288,512]{2,1,0:T(8,128)(2,1)} %shard_map.89), calls=%async_computation.1 | async-start | bytes 2359296 | tf_op jit(solution)/shard_map/all_to_all | solution.py:492
  112.2 0.1 pad_add_fusion.slot_of
  112.3 0.0 collective-permute-done.1.refs_1_
  112.3 1.6 collective-permute-done.2.refs_2_
  113.8 2.2 %collective-permute-done.3.refs_3_ = bf16[1024,1024]{1,0:T(8,128)(2,1)} collective-permute-done((bf16[1024,1024]{1,0:T(8,128)(2,1)S(1)}, bf16[1024,1024]{1,0:T(8,128)(2,1)}, u32[]{:S(2)}, u32[]{:S(2)}) %collective-permute-start.3) | collective-permute-done | bytes 2097184 | tf_op jit(solution)/shard_map/ppermute | solution.py:451
  116.0 6.9 %shard_map.88.mixed_hbm = f32[3,288,512]{2,1,0:T(8,128)} custom-call(s32[4]{0:T(128)S(1)} %pad_add_fusion.slot_of, s16[16,592,256]{2,1,0:T(8,128)(2,1)} %bitcast.18, bf16[1024,1024]{1,0:T(8,128)(2,1)S(1)} %pad_maximum_fusion.refs_0_, bf16[1024,1024]{1,0:T(8,128)(2,1)} %collective-permute-done.1.refs_1_, bf16[1024,1024]{1,0:T(8,128)(2,1)} %collective-permute-done.2.refs_2_, ...), custom_call_target="tpu_custom_call" | custom-call | flops 2415919104 | bytes 12582912 | tf_op jit(solution)/shard_map/pallas_call | solution.py:166
  122.9 2.0 %all-to-all-done.1.backs_hbm = bf16[4,288,512]{2,1,0:T(8,128)(2,1)S(1)} async-done(((bf16[4,288,512]{2,1,0:T(8,128)(2,1)}), bf16[4,288,512]{2,1,0:T(8,128)(2,1)S(1)}, u32[]{:S(2)}, u32[]{:S(2)}) %all-to-all-start.1) | async-done | bytes 1179680 | tf_op jit(solution)/shard_map/all_to_all | solution.py:492
  124.9 7.4 %shard_map.90 = bf16[5104,256]{1,0:T(8,128)(2,1)} custom-call(s32[4]{0:T(128)S(1)} %pad_add_fusion.slot_of, s32[1]{0:T(128)} %bitcast.8.z_of, f32[3,288,512]{2,1,0:T(8,128)} %shard_map.88.mixed_hbm, bf16[4,288,512]{2,1,0:T(8,128)(2,1)S(1)} %all-to-all-done.1.backs_hbm, bf16[1024,1024]{1,0:T(8,128)(2,1)S(1)} %pad_maximum_fusion.refs_0_, ...), custom_call_target="tpu_custom_call" | custom-call | flops 2415919104 | bytes 14680064 | tf_op jit(solution)/shard_map/pallas_call | solution.py:264
  132.3 0.0 copy-start.2
  132.3 33.9 %fusion = bf16[320,256]{1,0:T(8,128)(2,1)S(1)} fusion(bf16[5104,256]{1,0:T(8,128)(2,1)} %shard_map.90), kind=kCustom, calls=%all-reduce-scatter | all-reduce-scatter fusion | flops 1310721 | bytes 2779136
  166.2 2.5 %collective-permute-start.4 = (bf16[15,256]{1,0:T(8,128)(2,1)S(1)}, bf16[15,256]{1,0:T(8,128)(2,1)S(1)}, u32[]{:S(2)}, u32[]{:S(2)}) collective-permute-start(bf16[15,256]{1,0:T(8,128)(2,1)S(1)} %slice), channel_id=1, source_target_pairs={{0,4},{4,8},{8,12},{12,16},{16,20},{20,24},{24,28},{28,32},{32,36}... | collective-permute-start | bytes 23048
  168.6 1.3 dynamic-slice.4
  170.6 0.0 collective-permute-done.4
  170.6 0.5 concatenate.4
  171.1 0.7 constant_dynamic-slice_fusion.summed
  171.8 1.8 shard_map.91
  173.7 21.3 %all_to_all.15.came_hbm = bf16[8,48,256]{2,1,0:T(8,128)(2,1)S(1)} all-to-all(bf16[8,48,256]{2,1,0:T(8,128)(2,1)} %shard_map.91), channel_id=1, replica_groups=mesh['expert'=8,'etensor'=16,'dp'=4] {'expert'}, dimensions={0} | all-to-all | bytes 393216 | tf_op jit(solution)/shard_map/all_to_all | solution.py:507
  195.0 0.0 copy-done.2
  195.0 1.2 shard_map.92
  (1 shorter events, 0.0 us)
Async XLA Ops:
  0.6 0.8 copy-start.1
  2.2 26.9 %collective-permute-start = (bf16[144,256]{1,0:T(8,128)(2,1)S(1)}, bf16[144,256]{1,0:T(8,128)(2,1)S(1)}, u32[]{:S(2)}, u32[]{:S(2)}) collective-permute-start(bf16[144,256]{1,0:T(8,128)(2,1)S(1)} %shard_map.87), channel_id=1, source_target_pairs={{0,0},{1,16},{2,32},{3,48},{4,4},{5,20},{6,36},{7,52},{8,8},{9,24}... | collective-permute-start | bytes 221192 | tf_op jit(solution)/shard_map/ppermute | solution.py:475
  2.8 26.2 %copy-start.3 = (bf16[128,256]{1,0:T(8,128)(2,1)S(1)}, bf16[128,256]{1,0:T(8,128)(2,1)}, u32[]{:S(2)}) copy-start(bf16[128,256]{1,0:T(8,128)(2,1)} %param.9) | copy-start | bytes 196612
  2.8 26.2 %copy-start.4 = (s32[128,2]{0,1:T(2,128)S(1)}, s32[128,2]{0,1:T(2,128)}, u32[]{:S(2)}) copy-start(s32[128,2]{0,1:T(2,128)} %param.11) | copy-start | bytes 3076
  4.7 107.6 %collective-permute-start.1 = (bf16[1024,1024]{1,0:T(8,128)(2,1)S(1)}, bf16[1024,1024]{1,0:T(8,128)(2,1)}, u32[]{:S(2)}, u32[]{:S(2)}) collective-permute-start(bf16[1024,1024]{1,0:T(8,128)(2,1)S(1)} %pad_maximum_fusion.refs_0_), channel_id=1, source_target_pairs={{0,2},{1,3},{2,0},{3,1},{4,6},{5,7},{6,4},{7,5},{8,10},{9,11},{10,... | collective-permute-start | bytes 6291464 | tf_op jit(solution)/shard_map/ppermute | solution.py:451
  24.9 88.9 %collective-permute-start.2 = (bf16[1024,1024]{1,0:T(8,128)(2,1)S(1)}, bf16[1024,1024]{1,0:T(8,128)(2,1)}, u32[]{:S(2)}, u32[]{:S(2)}) collective-permute-start(bf16[1024,1024]{1,0:T(8,128)(2,1)S(1)} %pad_maximum_fusion.refs_0_), channel_id=1, source_target_pairs={{0,1},{1,0},{2,3},{3,2},{4,5},{5,4},{6,7},{7,6},{8,9},{9,8},{10,11... | collective-permute-start | bytes 6291464 | tf_op jit(solution)/shard_map/ppermute | solution.py:451
  26.8 89.2 %collective-permute-start.3 = (bf16[1024,1024]{1,0:T(8,128)(2,1)S(1)}, bf16[1024,1024]{1,0:T(8,128)(2,1)}, u32[]{:S(2)}, u32[]{:S(2)}) collective-permute-start(bf16[1024,1024]{1,0:T(8,128)(2,1)S(1)} %pad_maximum_fusion.refs_0_), channel_id=1, source_target_pairs={{0,3},{1,2},{2,1},{3,0},{4,7},{5,6},{6,5},{7,4},{8,11},{9,10},{10,... | collective-permute-start | bytes 6291464 | tf_op jit(solution)/shard_map/ppermute | solution.py:451
  43.6 60.4 %copy-start = (bf16[1,512,1024]{2,1,0:T(8,128)(2,1)S(1)}, bf16[1,512,1024]{2,1,0:T(8,128)(2,1)}, u32[]{:S(2)}) copy-start(bf16[1,512,1024]{2,1,0:T(8,128)(2,1)} %down.1) | copy-start | bytes 3145732
  108.0 16.9 %all-to-all-start.1 = ((bf16[4,288,512]{2,1,0:T(8,128)(2,1)}), bf16[4,288,512]{2,1,0:T(8,128)(2,1)S(1)}, u32[]{:S(2)}, u32[]{:S(2)}) async-start(bf16[4,288,512]{2,1,0:T(8,128)(2,1)} %shard_map.89), calls=%async_computation.1 | async-start | bytes 2359296 | tf_op jit(solution)/shard_map/all_to_all | solution.py:492
  132.3 62.7 %copy-start.2 = (f32[128,2]{0,1:T(2,128)S(1)}, f32[128,2]{0,1:T(2,128)}, u32[]{:S(2)}) copy-start(f32[128,2]{0,1:T(2,128)} %param.12) | copy-start | bytes 3076
  166.2 4.4 %collective-permute-start.4 = (bf16[15,256]{1,0:T(8,128)(2,1)S(1)}, bf16[15,256]{1,0:T(8,128)(2,1)S(1)}, u32[]{:S(2)}, u32[]{:S(2)}) collective-permute-start(bf16[15,256]{1,0:T(8,128)(2,1)S(1)} %slice), channel_id=1, source_target_pairs={{0,4},{4,8},{8,12},{12,16},{16,20},{20,24},{24,28},{28,32},{32,36}... | collective-permute-start | bytes 23048

commit v5 on v4

--- a/solution.py
+++ b/solution.py
@@ -208,6 +208,7 @@
         [(back * mixed[0]).astype(jnp.bfloat16), (back * mixed[1]).astype(jnp.bfloat16)], axis=1
     )
 
+    prod = sum(prod[:, 128 * i : 128 * (i + 1)] for i in range(prod.shape[1] // 128))
     ones = jnp.ones((16, prod.shape[1]), jnp.bfloat16)
     total = None
     rest = prod

time: 198 us -> 197 us (level)
  no operation moved by 1% of the time
where the time goes in v5:
time: 197 us; the launch traced here: 196 us
  blocking collectives  129 us (65%)
  starting transfers between devices  31.6 us (16%)
  Pallas kernels  22.4 us (11%)
  waiting for transfers between devices  5.74 us (3%)
  local copies, waits for them, and re-layouts  3.38 us (2%)
    all_gather x1, blocking collectives, shards(): coded = lax.all_gather(coded, 'etensor', axis=0, tiled=False)  60.4 us
    unnamed x1, blocking collectives  33.9 us
    ppermute x3, starting transfers between devices, trade(): lax.ppermute(value, axis, [(i, i ^ bits) for i in range(lax.axis_size(axi...  24.3 us
    all_to_all x1, blocking collectives, shards(): lax.all_to_all(payload, 'expert', split_axis=0, concat_axis=0, tiled=True)  21.3 us
    all_to_all x1, blocking collectives, send(): lax.all_to_all(placed, 'expert', split_axis=0, concat_axis=0, tiled=True)  13.6 us
    pallas_call x1, Pallas kernels, term_part(): pl.pallas_call(functools.partial(term_kernel, pitch, slots), out_shape=pl...  6.95 us
    pallas_call x1, Pallas kernels, hidden_part(): pl.pallas_call(functools.partial(hidden_kernel, cap_rows), out_shape=pltp...  6.86 us
    all_to_all x1, starting transfers between devices, shards(): lax.all_to_all(back_parts(coded, down_weight, cap_rows, columns), 'dp', s...  4.21 us
  transfers between devices with their start and end apart: 6, of which 3 were waited for; matrix products, arithmetic and copies ran while one was open for 2% of the time, Pallas kernels for 6%

profile of v5, /device:TPU:1, one launch (start us, length us, event | category | flops | bytes accessed | tf_op | source)
XLA Modules:
  0.0 195.7 jit_solution(7580670391344337084)
XLA Ops:
  0.6 0.0 copy-start.1
  0.6 0.8 copy-done.1
  1.5 0.7 shard_map.87
  2.2 0.7 collective-permute-start
  2.8 0.0 copy-start.3
  2.8 0.0 copy-start.4
  2.8 1.8 pad_maximum_fusion.refs_0_
  4.7 20.2 %collective-permute-start.1 = (bf16[1024,1024]{1,0:T(8,128)(2,1)S(1)}, bf16[1024,1024]{1,0:T(8,128)(2,1)}, u32[]{:S(2)}, u32[]{:S(2)}) collective-permute-start(bf16[1024,1024]{1,0:T(8,128)(2,1)S(1)} %pad_maximum_fusion.refs_0_), channel_id=1, source_target_pairs={{0,2},{1,3},{2,0},{3,1},{4,6},{5,7},{6,4},{7,5},{8,10},{9,11},{10,... | collective-permute-start | bytes 6291464 | tf_op jit(solution)/shard_map/ppermute | solution.py:452
  24.9 1.9 collective-permute-start.2
  26.8 2.2 %collective-permute-start.3 = (bf16[1024,1024]{1,0:T(8,128)(2,1)S(1)}, bf16[1024,1024]{1,0:T(8,128)(2,1)}, u32[]{:S(2)}, u32[]{:S(2)}) collective-permute-start(bf16[1024,1024]{1,0:T(8,128)(2,1)S(1)} %pad_maximum_fusion.refs_0_), channel_id=1, source_target_pairs={{0,3},{1,2},{2,1},{3,0},{4,7},{5,6},{6,5},{7,4},{8,11},{9,10},{10,... | collective-permute-start | bytes 6291464 | tf_op jit(solution)/shard_map/ppermute | solution.py:452
  29.0 0.0 collective-permute-done
  29.0 0.0 copy-done.3
  29.1 0.0 copy-done.4
  29.1 14.5 %conditional.1 = (s16[592,256]{1,0:T(8,128)(2,1)S(1)}, s32[2,128]{1,0:T(2,128)S(1)}) conditional(s32[]{:T(128)} %convert_element_type.3, () %tuple.16, (s32[128,2]{0,1:T(2,128)S(1)}, bf16[128,256]{1,0:T(8,128)(2,1)S(1)}, bf16[144,256]{1,0:T(8,128)(2,1)S(1)}) %tuple.22), branch_computations={%region_0.0_spmd, %region_1.0_spmd} | conditional | bytes 589840 | solution.py:483
  29.1 0.5 branch_1_fun.2
  29.6 13.6 %all_to_all.14.rows_hbm = bf16[8,36,512]{2,1,0:T(8,128)(2,1)S(1)} all-to-all(bf16[8,36,512]{2,1,0:T(8,128)(2,1)S(1)} %get-tuple-element.9), channel_id=1, replica_groups=mesh['expert'=8,'etensor'=16,'dp'=4] {'expert'}, dimensions={0} | all-to-all | bytes 589824 | tf_op jit(solution)/shard_map/cond/branch_1_fun/all_to_all | solution.py:480
  43.2 0.3 branch_1_fun.3
  43.6 0.0 copy-start
  43.6 60.4 %all-gather.2 = s16[9472,256]{1,0:T(8,128)(2,1)} all-gather(s16[592,256]{1,0:T(8,128)(2,1)S(1)} %get-tuple-element.18), channel_id=2, replica_groups=mesh['expert'=8,'etensor'=16,'dp'=4] {'etensor'}, dimensions={0}, use_global_device_ids=true | all-gather | bytes 5152768 | tf_op jit(solution)/shard_map/all_gather | solution.py:491
  104.0 0.0 copy-done
  104.0 4.0 %shard_map.89 = bf16[4,288,512]{2,1,0:T(8,128)(2,1)} custom-call(s16[16,592,256]{2,1,0:T(8,128)(2,1)} %bitcast.17, bf16[1,512,1024]{2,1,0:T(8,128)(2,1)S(1)} %copy-done), custom_call_target="tpu_custom_call" | custom-call | flops 1207959552 | bytes 5242880 | tf_op jit(solution)/shard_map/pallas_call | solution.py:109
  108.0 4.2 %all-to-all-start.1 = ((bf16[4,288,512]{2,1,0:T(8,128)(2,1)}), bf16[4,288,512]{2,1,0:T(8,128)(2,1)S(1)}, u32[]{:S(2)}, u32[]{:S(2)}) async-start(bf16[4,288,512]{2,1,0:T(8,128)(2,1)} %shard_map.89), calls=%async_computation.1 | async-start | bytes 2359296 | tf_op jit(solution)/shard_map/all_to_all | solution.py:493
  112.2 0.1 pad_add_fusion.slot_of
  112.3 0.0 collective-permute-done.1.refs_1_
  112.3 1.6 collective-permute-done.2.refs_2_
  113.8 2.2 %collective-permute-done.3.refs_3_ = bf16[1024,1024]{1,0:T(8,128)(2,1)} collective-permute-done((bf16[1024,1024]{1,0:T(8,128)(2,1)S(1)}, bf16[1024,1024]{1,0:T(8,128)(2,1)}, u32[]{:S(2)}, u32[]{:S(2)}) %collective-permute-start.3) | collective-permute-done | bytes 2097184 | tf_op jit(solution)/shard_map/ppermute | solution.py:452
  116.0 6.9 %shard_map.88.mixed_hbm = f32[3,288,512]{2,1,0:T(8,128)} custom-call(s32[4]{0:T(128)S(1)} %pad_add_fusion.slot_of, s16[16,592,256]{2,1,0:T(8,128)(2,1)} %bitcast.18, bf16[1024,1024]{1,0:T(8,128)(2,1)S(1)} %pad_maximum_fusion.refs_0_, bf16[1024,1024]{1,0:T(8,128)(2,1)} %collective-permute-done.1.refs_1_, bf16[1024,1024]{1,0:T(8,128)(2,1)} %collective-permute-done.2.refs_2_, ...), custom_call_target="tpu_custom_call" | custom-call | flops 2415919104 | bytes 12582912 | tf_op jit(solution)/shard_map/pallas_call | solution.py:166
  122.9 2.0 %all-to-all-done.1.backs_hbm = bf16[4,288,512]{2,1,0:T(8,128)(2,1)S(1)} async-done(((bf16[4,288,512]{2,1,0:T(8,128)(2,1)}), bf16[4,288,512]{2,1,0:T(8,128)(2,1)S(1)}, u32[]{:S(2)}, u32[]{:S(2)}) %all-to-all-start.1) | async-done | bytes 1179680 | tf_op jit(solution)/shard_map/all_to_all | solution.py:493
  124.9 7.0 %shard_map.90 = bf16[5104,256]{1,0:T(8,128)(2,1)} custom-call(s32[4]{0:T(128)S(1)} %pad_add_fusion.slot_of, s32[1]{0:T(128)} %bitcast.8.z_of, f32[3,288,512]{2,1,0:T(8,128)} %shard_map.88.mixed_hbm, bf16[4,288,512]{2,1,0:T(8,128)(2,1)S(1)} %all-to-all-done.1.backs_hbm, bf16[1024,1024]{1,0:T(8,128)(2,1)S(1)} %pad_maximum_fusion.refs_0_, ...), custom_call_target="tpu_custom_call" | custom-call | flops 2415919104 | bytes 14680064 | tf_op jit(solution)/shard_map/pallas_call | solution.py:265
  131.8 0.0 copy-start.2
  131.9 33.9 %fusion = bf16[320,256]{1,0:T(8,128)(2,1)S(1)} fusion(bf16[5104,256]{1,0:T(8,128)(2,1)} %shard_map.90), kind=kCustom, calls=%all-reduce-scatter | all-reduce-scatter fusion | flops 1310721 | bytes 2779136
  165.7 2.5 %collective-permute-start.4 = (bf16[15,256]{1,0:T(8,128)(2,1)S(1)}, bf16[15,256]{1,0:T(8,128)(2,1)S(1)}, u32[]{:S(2)}, u32[]{:S(2)}) collective-permute-start(bf16[15,256]{1,0:T(8,128)(2,1)S(1)} %slice), channel_id=1, source_target_pairs={{0,4},{4,8},{8,12},{12,16},{16,20},{20,24},{24,28},{28,32},{32,36}... | collective-permute-start | bytes 23048
  168.2 1.3 dynamic-slice.4
  170.1 0.0 collective-permute-done.4
  170.1 0.5 concatenate.4
  170.7 0.7 constant_dynamic-slice_fusion.summed
  171.4 1.8 shard_map.91
  173.2 21.3 %all_to_all.15.came_hbm = bf16[8,48,256]{2,1,0:T(8,128)(2,1)S(1)} all-to-all(bf16[8,48,256]{2,1,0:T(8,128)(2,1)} %shard_map.91), channel_id=1, replica_groups=mesh['expert'=8,'etensor'=16,'dp'=4] {'expert'}, dimensions={0} | all-to-all | bytes 393216 | tf_op jit(solution)/shard_map/all_to_all | solution.py:508
  194.5 0.0 copy-done.2
  194.5 1.2 shard_map.92
  (1 shorter events, 0.0 us)
Async XLA Ops:
  0.6 0.8 copy-start.1
  2.2 26.9 %collective-permute-start = (bf16[144,256]{1,0:T(8,128)(2,1)S(1)}, bf16[144,256]{1,0:T(8,128)(2,1)S(1)}, u32[]{:S(2)}, u32[]{:S(2)}) collective-permute-start(bf16[144,256]{1,0:T(8,128)(2,1)S(1)} %shard_map.87), channel_id=1, source_target_pairs={{0,0},{1,16},{2,32},{3,48},{4,4},{5,20},{6,36},{7,52},{8,8},{9,24}... | collective-permute-start | bytes 221192 | tf_op jit(solution)/shard_map/ppermute | solution.py:476
  2.8 26.2 %copy-start.3 = (bf16[128,256]{1,0:T(8,128)(2,1)S(1)}, bf16[128,256]{1,0:T(8,128)(2,1)}, u32[]{:S(2)}) copy-start(bf16[128,256]{1,0:T(8,128)(2,1)} %param.9) | copy-start | bytes 196612
  2.8 26.2 %copy-start.4 = (s32[128,2]{0,1:T(2,128)S(1)}, s32[128,2]{0,1:T(2,128)}, u32[]{:S(2)}) copy-start(s32[128,2]{0,1:T(2,128)} %param.11) | copy-start | bytes 3076
  4.7 107.6 %collective-permute-start.1 = (bf16[1024,1024]{1,0:T(8,128)(2,1)S(1)}, bf16[1024,1024]{1,0:T(8,128)(2,1)}, u32[]{:S(2)}, u32[]{:S(2)}) collective-permute-start(bf16[1024,1024]{1,0:T(8,128)(2,1)S(1)} %pad_maximum_fusion.refs_0_), channel_id=1, source_target_pairs={{0,2},{1,3},{2,0},{3,1},{4,6},{5,7},{6,4},{7,5},{8,10},{9,11},{10,... | collective-permute-start | bytes 6291464 | tf_op jit(solution)/shard_map/ppermute | solution.py:452
  24.9 88.9 %collective-permute-start.2 = (bf16[1024,1024]{1,0:T(8,128)(2,1)S(1)}, bf16[1024,1024]{1,0:T(8,128)(2,1)}, u32[]{:S(2)}, u32[]{:S(2)}) collective-permute-start(bf16[1024,1024]{1,0:T(8,128)(2,1)S(1)} %pad_maximum_fusion.refs_0_), channel_id=1, source_target_pairs={{0,1},{1,0},{2,3},{3,2},{4,5},{5,4},{6,7},{7,6},{8,9},{9,8},{10,11... | collective-permute-start | bytes 6291464 | tf_op jit(solution)/shard_map/ppermute | solution.py:452
  26.8 89.2 %collective-permute-start.3 = (bf16[1024,1024]{1,0:T(8,128)(2,1)S(1)}, bf16[1024,1024]{1,0:T(8,128)(2,1)}, u32[]{:S(2)}, u32[]{:S(2)}) collective-permute-start(bf16[1024,1024]{1,0:T(8,128)(2,1)S(1)} %pad_maximum_fusion.refs_0_), channel_id=1, source_target_pairs={{0,3},{1,2},{2,1},{3,0},{4,7},{5,6},{6,5},{7,4},{8,11},{9,10},{10,... | collective-permute-start | bytes 6291464 | tf_op jit(solution)/shard_map/ppermute | solution.py:452
  43.6 60.4 %copy-start = (bf16[1,512,1024]{2,1,0:T(8,128)(2,1)S(1)}, bf16[1,512,1024]{2,1,0:T(8,128)(2,1)}, u32[]{:S(2)}) copy-start(bf16[1,512,1024]{2,1,0:T(8,128)(2,1)} %down.1) | copy-start | bytes 3145732
  108.0 16.9 %all-to-all-start.1 = ((bf16[4,288,512]{2,1,0:T(8,128)(2,1)}), bf16[4,288,512]{2,1,0:T(8,128)(2,1)S(1)}, u32[]{:S(2)}, u32[]{:S(2)}) async-start(bf16[4,288,512]{2,1,0:T(8,128)(2,1)} %shard_map.89), calls=%async_computation.1 | async-start | bytes 2359296 | tf_op jit(solution)/shard_map/all_to_all | solution.py:493
  131.8 62.7 %copy-start.2 = (f32[128,2]{0,1:T(2,128)S(1)}, f32[128,2]{0,1:T(2,128)}, u32[]{:S(2)}) copy-start(f32[128,2]{0,1:T(2,128)} %param.12) | copy-start | bytes 3076
  165.7 4.4 %collective-permute-start.4 = (bf16[15,256]{1,0:T(8,128)(2,1)S(1)}, bf16[15,256]{1,0:T(8,128)(2,1)S(1)}, u32[]{:S(2)}, u32[]{:S(2)}) collective-permute-start(bf16[15,256]{1,0:T(8,128)(2,1)S(1)} %slice), channel_id=1, source_target_pairs={{0,4},{4,8},{8,12},{12,16},{16,20},{20,24},{24,28},{28,32},{32,36}... | collective-permute-start | bytes 23048

commit v6 on v5

--- a/solution.py
+++ b/solution.py
@@ -300,7 +300,7 @@
         in_specs=[VMEM, VMEM],
         out_specs=VMEM,
         compiler_params=pltpu.CompilerParams(vmem_limit_bytes=8 << 20),
-    )(out_grad, routes)
+    )(pltpu.with_memory_space_constraint(out_grad, pltpu.HBM), routes)
 
 
 def place_kernel(capacity, routes, tokens, moved_hbm, placed, slot, moved, sem):

time: 197 us -> 196 us (level)
  no operation moved by 1% of the time
where the time goes in v6:
time: 196 us; the launch traced here: 195 us
  blocking collectives  129 us (66%)
  starting transfers between devices  31.7 us (16%)
  Pallas kernels  22.5 us (11%)
  waiting for transfers between devices  5.7 us (3%)
  local copies, waits for them, and re-layouts  2.55 us (1%)
    all_gather x1, blocking collectives, shards(): coded = lax.all_gather(coded, 'etensor', axis=0, tiled=False)  60.4 us
    unnamed x1, blocking collectives  33.8 us
    ppermute x3, starting transfers between devices, trade(): lax.ppermute(value, axis, [(i, i ^ bits) for i in range(lax.axis_size(axi...  24.3 us
    all_to_all x1, blocking collectives, shards(): lax.all_to_all(payload, 'expert', split_axis=0, concat_axis=0, tiled=True)  21.4 us
    all_to_all x1, blocking collectives, send(): lax.all_to_all(placed, 'expert', split_axis=0, concat_axis=0, tiled=True)  13.7 us
    pallas_call x1, Pallas kernels, term_part(): pl.pallas_call(functools.partial(term_kernel, pitch, slots), out_shape=pl...  6.94 us
    pallas_call x1, Pallas kernels, hidden_part(): pl.pallas_call(functools.partial(hidden_kernel, cap_rows), out_shape=pltp...  6.86 us
    all_to_all x1, starting transfers between devices, shards(): lax.all_to_all(back_parts(coded, down_weight, cap_rows, columns), 'dp', s...  4.23 us
  transfers between devices with their start and end apart: 6, of which 3 were waited for; matrix products, arithmetic and copies ran while one was open for 2% of the time, Pallas kernels for 6%

profile of v6, /device:TPU:1, one launch (start us, length us, event | category | flops | bytes accessed | tf_op | source)
XLA Modules:
  0.0 195.1 jit_solution(12907774664090943499)
XLA Ops:
  0.6 0.9 shard_map.87
  1.5 0.7 collective-permute-start
  2.2 0.0 copy-start.2
  2.2 0.0 copy-start.3
  2.2 1.8 pad_maximum_fusion.refs_0_
  4.0 20.2 %collective-permute-start.1 = (bf16[1024,1024]{1,0:T(8,128)(2,1)S(1)}, bf16[1024,1024]{1,0:T(8,128)(2,1)}, u32[]{:S(2)}, u32[]{:S(2)}) collective-permute-start(bf16[1024,1024]{1,0:T(8,128)(2,1)S(1)} %pad_maximum_fusion.refs_0_), channel_id=1, source_target_pairs={{0,2},{1,3},{2,0},{3,1},{4,6},{5,7},{6,4},{7,5},{8,10},{9,11},{10,... | collective-permute-start | bytes 6291464 | tf_op jit(solution)/shard_map/ppermute | solution.py:452
  24.2 1.9 collective-permute-start.2
  26.2 2.2 %collective-permute-start.3 = (bf16[1024,1024]{1,0:T(8,128)(2,1)S(1)}, bf16[1024,1024]{1,0:T(8,128)(2,1)}, u32[]{:S(2)}, u32[]{:S(2)}) collective-permute-start(bf16[1024,1024]{1,0:T(8,128)(2,1)S(1)} %pad_maximum_fusion.refs_0_), channel_id=1, source_target_pairs={{0,3},{1,2},{2,1},{3,0},{4,7},{5,6},{6,5},{7,4},{8,11},{9,10},{10,... | collective-permute-start | bytes 6291464 | tf_op jit(solution)/shard_map/ppermute | solution.py:452
  28.4 0.0 collective-permute-done
  28.4 0.0 copy-done.2
  28.4 0.0 copy-done.3
  28.4 14.5 %conditional.1 = (s16[592,256]{1,0:T(8,128)(2,1)S(1)}, s32[2,128]{1,0:T(2,128)S(1)}) conditional(s32[]{:T(128)} %convert_element_type.3, () %tuple.16, (s32[128,2]{0,1:T(2,128)S(1)}, bf16[128,256]{1,0:T(8,128)(2,1)S(1)}, bf16[144,256]{1,0:T(8,128)(2,1)S(1)}) %tuple.22), branch_computations={%region_0.0_spmd, %region_1.0_spmd} | conditional | bytes 589840 | solution.py:483
  28.4 0.5 branch_1_fun.2
  28.9 13.7 %all_to_all.14.rows_hbm = bf16[8,36,512]{2,1,0:T(8,128)(2,1)S(1)} all-to-all(bf16[8,36,512]{2,1,0:T(8,128)(2,1)S(1)} %get-tuple-element.9), channel_id=1, replica_groups=mesh['expert'=8,'etensor'=16,'dp'=4] {'expert'}, dimensions={0} | all-to-all | bytes 589824 | tf_op jit(solution)/shard_map/cond/branch_1_fun/all_to_all | solution.py:480
  42.6 0.3 branch_1_fun.3
  42.9 0.0 copy-start
  42.9 60.4 %all-gather.2 = s16[9472,256]{1,0:T(8,128)(2,1)} all-gather(s16[592,256]{1,0:T(8,128)(2,1)S(1)} %get-tuple-element.18), channel_id=2, replica_groups=mesh['expert'=8,'etensor'=16,'dp'=4] {'etensor'}, dimensions={0}, use_global_device_ids=true | all-gather | bytes 5152768 | tf_op jit(solution)/shard_map/all_gather | solution.py:491
  103.3 0.0 copy-done
  103.3 4.0 %shard_map.89 = bf16[4,288,512]{2,1,0:T(8,128)(2,1)} custom-call(s16[16,592,256]{2,1,0:T(8,128)(2,1)} %bitcast.17, bf16[1,512,1024]{2,1,0:T(8,128)(2,1)S(1)} %copy-done), custom_call_target="tpu_custom_call" | custom-call | flops 1207959552 | bytes 5242880 | tf_op jit(solution)/shard_map/pallas_call | solution.py:109
  107.3 4.2 %all-to-all-start.1 = ((bf16[4,288,512]{2,1,0:T(8,128)(2,1)}), bf16[4,288,512]{2,1,0:T(8,128)(2,1)S(1)}, u32[]{:S(2)}, u32[]{:S(2)}) async-start(bf16[4,288,512]{2,1,0:T(8,128)(2,1)} %shard_map.89), calls=%async_computation.1 | async-start | bytes 2359296 | tf_op jit(solution)/shard_map/all_to_all | solution.py:493
  111.6 0.1 pad_add_fusion.slot_of
  111.6 0.0 collective-permute-done.1.refs_1_
  111.6 1.5 collective-permute-done.2.refs_2_
  113.2 2.2 %collective-permute-done.3.refs_3_ = bf16[1024,1024]{1,0:T(8,128)(2,1)} collective-permute-done((bf16[1024,1024]{1,0:T(8,128)(2,1)S(1)}, bf16[1024,1024]{1,0:T(8,128)(2,1)}, u32[]{:S(2)}, u32[]{:S(2)}) %collective-permute-start.3) | collective-permute-done | bytes 2097184 | tf_op jit(solution)/shard_map/ppermute | solution.py:452
  115.4 6.9 %shard_map.88.mixed_hbm = f32[3,288,512]{2,1,0:T(8,128)} custom-call(s32[4]{0:T(128)S(1)} %pad_add_fusion.slot_of, s16[16,592,256]{2,1,0:T(8,128)(2,1)} %bitcast.18, bf16[1024,1024]{1,0:T(8,128)(2,1)S(1)} %pad_maximum_fusion.refs_0_, bf16[1024,1024]{1,0:T(8,128)(2,1)} %collective-permute-done.1.refs_1_, bf16[1024,1024]{1,0:T(8,128)(2,1)} %collective-permute-done.2.refs_2_, ...), custom_call_target="tpu_custom_call" | custom-call | flops 2415919104 | bytes 12582912 | tf_op jit(solution)/shard_map/pallas_call | solution.py:166
  122.2 2.0 %all-to-all-done.1.backs_hbm = bf16[4,288,512]{2,1,0:T(8,128)(2,1)S(1)} async-done(((bf16[4,288,512]{2,1,0:T(8,128)(2,1)}), bf16[4,288,512]{2,1,0:T(8,128)(2,1)S(1)}, u32[]{:S(2)}, u32[]{:S(2)}) %all-to-all-start.1) | async-done | bytes 1179680 | tf_op jit(solution)/shard_map/all_to_all | solution.py:493
  124.2 6.9 %shard_map.90 = bf16[5104,256]{1,0:T(8,128)(2,1)} custom-call(s32[4]{0:T(128)S(1)} %pad_add_fusion.slot_of, s32[1]{0:T(128)} %bitcast.8.z_of, f32[3,288,512]{2,1,0:T(8,128)} %shard_map.88.mixed_hbm, bf16[4,288,512]{2,1,0:T(8,128)(2,1)S(1)} %all-to-all-done.1.backs_hbm, bf16[1024,1024]{1,0:T(8,128)(2,1)S(1)} %pad_maximum_fusion.refs_0_, ...), custom_call_target="tpu_custom_call" | custom-call | flops 2415919104 | bytes 14680064 | tf_op jit(solution)/shard_map/pallas_call | solution.py:265
  131.1 0.0 copy-start.1
  131.2 33.8 %fusion = bf16[320,256]{1,0:T(8,128)(2,1)S(1)} fusion(bf16[5104,256]{1,0:T(8,128)(2,1)} %shard_map.90), kind=kCustom, calls=%all-reduce-scatter | all-reduce-scatter fusion | flops 1310721 | bytes 2779136
  164.9 2.5 %collective-permute-start.4 = (bf16[15,256]{1,0:T(8,128)(2,1)S(1)}, bf16[15,256]{1,0:T(8,128)(2,1)S(1)}, u32[]{:S(2)}, u32[]{:S(2)}) collective-permute-start(bf16[15,256]{1,0:T(8,128)(2,1)S(1)} %slice), channel_id=1, source_target_pairs={{0,4},{4,8},{8,12},{12,16},{16,20},{20,24},{24,28},{28,32},{32,36}... | collective-permute-start | bytes 23048
  167.4 1.3 dynamic-slice.4
  169.3 0.0 collective-permute-done.4
  169.3 0.5 concatenate.4
  169.9 0.7 constant_dynamic-slice_fusion.summed
  170.6 1.8 shard_map.91
  172.4 21.4 %all_to_all.15.came_hbm = bf16[8,48,256]{2,1,0:T(8,128)(2,1)S(1)} all-to-all(bf16[8,48,256]{2,1,0:T(8,128)(2,1)} %shard_map.91), channel_id=1, replica_groups=mesh['expert'=8,'etensor'=16,'dp'=4] {'expert'}, dimensions={0} | all-to-all | bytes 393216 | tf_op jit(solution)/shard_map/all_to_all | solution.py:508
  193.9 0.0 copy-done.1
  193.9 1.2 shard_map.92
  (1 shorter events, 0.0 us)
Async XLA Ops:
  1.5 26.9 %collective-permute-start = (bf16[144,256]{1,0:T(8,128)(2,1)S(1)}, bf16[144,256]{1,0:T(8,128)(2,1)S(1)}, u32[]{:S(2)}, u32[]{:S(2)}) collective-permute-start(bf16[144,256]{1,0:T(8,128)(2,1)S(1)} %shard_map.87), channel_id=1, source_target_pairs={{0,0},{1,16},{2,32},{3,48},{4,4},{5,20},{6,36},{7,52},{8,8},{9,24}... | collective-permute-start | bytes 221192 | tf_op jit(solution)/shard_map/ppermute | solution.py:476
  2.2 26.2 %copy-start.2 = (bf16[128,256]{1,0:T(8,128)(2,1)S(1)}, bf16[128,256]{1,0:T(8,128)(2,1)}, u32[]{:S(2)}) copy-start(bf16[128,256]{1,0:T(8,128)(2,1)} %param.9) | copy-start | bytes 196612
  2.2 26.2 %copy-start.3 = (s32[128,2]{0,1:T(2,128)S(1)}, s32[128,2]{0,1:T(2,128)}, u32[]{:S(2)}) copy-start(s32[128,2]{0,1:T(2,128)} %param.11) | copy-start | bytes 3076
  4.0 107.6 %collective-permute-start.1 = (bf16[1024,1024]{1,0:T(8,128)(2,1)S(1)}, bf16[1024,1024]{1,0:T(8,128)(2,1)}, u32[]{:S(2)}, u32[]{:S(2)}) collective-permute-start(bf16[1024,1024]{1,0:T(8,128)(2,1)S(1)} %pad_maximum_fusion.refs_0_), channel_id=1, source_target_pairs={{0,2},{1,3},{2,0},{3,1},{4,6},{5,7},{6,4},{7,5},{8,10},{9,11},{10,... | collective-permute-start | bytes 6291464 | tf_op jit(solution)/shard_map/ppermute | solution.py:452
  24.2 88.9 %collective-permute-start.2 = (bf16[1024,1024]{1,0:T(8,128)(2,1)S(1)}, bf16[1024,1024]{1,0:T(8,128)(2,1)}, u32[]{:S(2)}, u32[]{:S(2)}) collective-permute-start(bf16[1024,1024]{1,0:T(8,128)(2,1)S(1)} %pad_maximum_fusion.refs_0_), channel_id=1, source_target_pairs={{0,1},{1,0},{2,3},{3,2},{4,5},{5,4},{6,7},{7,6},{8,9},{9,8},{10,11... | collective-permute-start | bytes 6291464 | tf_op jit(solution)/shard_map/ppermute | solution.py:452
  26.2 89.2 %collective-permute-start.3 = (bf16[1024,1024]{1,0:T(8,128)(2,1)S(1)}, bf16[1024,1024]{1,0:T(8,128)(2,1)}, u32[]{:S(2)}, u32[]{:S(2)}) collective-permute-start(bf16[1024,1024]{1,0:T(8,128)(2,1)S(1)} %pad_maximum_fusion.refs_0_), channel_id=1, source_target_pairs={{0,3},{1,2},{2,1},{3,0},{4,7},{5,6},{6,5},{7,4},{8,11},{9,10},{10,... | collective-permute-start | bytes 6291464 | tf_op jit(solution)/shard_map/ppermute | solution.py:452
  42.9 60.4 %copy-start = (bf16[1,512,1024]{2,1,0:T(8,128)(2,1)S(1)}, bf16[1,512,1024]{2,1,0:T(8,128)(2,1)}, u32[]{:S(2)}) copy-start(bf16[1,512,1024]{2,1,0:T(8,128)(2,1)} %down.1) | copy-start | bytes 3145732
  107.3 16.9 %all-to-all-start.1 = ((bf16[4,288,512]{2,1,0:T(8,128)(2,1)}), bf16[4,288,512]{2,1,0:T(8,128)(2,1)S(1)}, u32[]{:S(2)}, u32[]{:S(2)}) async-start(bf16[4,288,512]{2,1,0:T(8,128)(2,1)} %shard_map.89), calls=%async_computation.1 | async-start | bytes 2359296 | tf_op jit(solution)/shard_map/all_to_all | solution.py:493
  131.1 62.7 %copy-start.1 = (f32[128,2]{0,1:T(2,128)S(1)}, f32[128,2]{0,1:T(2,128)}, u32[]{:S(2)}) copy-start(f32[128,2]{0,1:T(2,128)} %param.12) | copy-start | bytes 3076
  164.9 4.4 %collective-permute-start.4 = (bf16[15,256]{1,0:T(8,128)(2,1)S(1)}, bf16[15,256]{1,0:T(8,128)(2,1)S(1)}, u32[]{:S(2)}, u32[]{:S(2)}) collective-permute-start(bf16[15,256]{1,0:T(8,128)(2,1)S(1)} %slice), channel_id=1, source_target_pairs={{0,4},{4,8},{8,12},{12,16},{16,20},{20,24},{24,28},{28,32},{32,36}... | collective-permute-start | bytes 23048
